TPU v7x, 32 devices: a whole 2x2x4 slice. The times are simulated.
32 devices in a mesh: dp: 8 (over z, x), tensor: 2 (over core), group: 2 (over y).
Axes of the slice: x: 2, y: 2, z: 4, core: 2. Of those that a mesh axis runs over, the one named last changes fastest.
Arguments:
- ref_image: bfloat16 [1024, 768], P(('dp', 'tensor')), may hold values from -100 to 100
- ref_text: bfloat16 [1024, 768], P(('dp', 'tensor')), may hold values from -100 to 100
- learner_image: bfloat16 [1024, 1024], P(('dp', 'tensor')), may hold values from -100 to 100
- learner_text: bfloat16 [1024, 1024], P(('dp', 'tensor')), may hold values from -100 to 100
- patches: bfloat16 [1024, 16, 1024], P('dp', 'group', 'tensor'), may hold values from -6 to 6
- cotangent: bfloat16 [1024, 16, 1024], P('dp', 'group', 'tensor'), may hold values from -6 to 6
- w_up: bfloat16 [1024, 4096], P(None, 'tensor'), may hold values from -0.1875 to 0.1875
- w_down: bfloat16 [4096, 1024], P('tensor'), may hold values from -0.09375 to 0.09375
- counts: int32 [8], P('dp'), may hold values from 1 to 64, 384 in all
- sel_index: int32 [512], P('dp'), may hold values from 0 to 127, as said below
- sel_dest: int32 [512, 1], P('dp'), may hold values from 0 to 7; in each aligned block of 64 rows (0 to 63, 64 to 127, ...) at most 16 rows name the same one
Outputs:
- learnability: float32 [1024], P(('dp', 'tensor'))
- routed_out: bfloat16 [1024, 16, 1024], P('dp', 'group', 'tensor')
- grad_up: float32 [1024, 4096], P(('dp', 'group'), 'tensor')
- grad_down_t: float32 [1024, 4096], P(('dp', 'group'), 'tensor')
Inputs may be any that keep to these rules, and one draw needn't show every extreme that they name: `sel_index`: within each aligned block of 64 entries the positions are distinct. `sel_dest`: within each aligned block of 64 rows no shard is named more than 16 times.
All inputs are finite; a program needn't handle non-finite values. No bound on the sum of `counts` on one device may be relied on, other than what follows from the above.
Results may differ from a plain program's by a relative error of at most 0.012.
Values may be sent and summed in bfloat16 or wider, within the bound.
A program may use at most 128 MiB of HBM per device.

v0:
```python
import jax
import jax.numpy as jnp
from jax import lax
from jax.sharding import PartitionSpec as P


def partner_2(block, axis, apart):
    count = lax.axis_size(axis)
    route = []
    for low in range(count):
        high = low | 1 << apart
        if high != low and high < count:
            route += [(low, high), (high, low)]
    return lax.ppermute(block, axis, route)


def unit_rows(block):
    wide = block.astype(jnp.float32)
    return (wide * lax.rsqrt(jnp.sum(wide * wide, axis=1, keepdims=True) + 1e-06)).astype(
        jnp.bfloat16
    )


def pair_losses(image, text, temp, bias):
    unit_img = unit_rows(image)
    unit_txt = unit_rows(text)
    rows = unit_img.shape[0]
    first = (lax.axis_index("dp") * lax.axis_size("tensor") + lax.axis_index("tensor")) * rows
    own = first + jnp.arange(rows, dtype=jnp.int32)
    far_img = lax.all_gather(unit_img, ("dp", "tensor"), axis=0, tiled=True)
    far_txt = lax.all_gather(unit_txt, ("dp", "tensor"), axis=0, tiled=True)
    count = far_img.shape[0]
    other = jnp.arange(count, dtype=jnp.int32)
    same = own[:, None] == other[None, :]
    img_scores = (
        temp * jnp.einsum("rd,kd->rk", unit_img, far_txt, preferred_element_type=jnp.float32) + bias
    )
    txt_scores = (
        temp * jnp.einsum("rd,kd->rk", unit_txt, far_img, preferred_element_type=jnp.float32) + bias
    )
    img_terms = jnp.where(same, jax.nn.softplus(-img_scores), jax.nn.softplus(img_scores))
    txt_terms = jnp.where(same, jax.nn.softplus(-txt_scores), jax.nn.softplus(txt_scores))
    img_loss = jnp.sum(img_terms, axis=1)
    txt_loss = jnp.sum(txt_terms, axis=1)
    return 0.5 * (img_loss + txt_loss)


def widen(half_x, half_scaled):
    return (
        lax.all_gather(half_x, "tensor", axis=2, tiled=True),
        lax.all_gather(half_scaled, "tensor", axis=2, tiled=True),
    )


def layer(wide_x, wide_scaled, half_x, w_up, w_down):
    items, patch_rows, width = wide_x.shape
    count = items * patch_rows
    flat = wide_x.reshape(count, width)
    scaled = wide_scaled.reshape(count, width)
    pre = jnp.dot(flat, w_up, preferred_element_type=jnp.float32)
    act_full, gelu_back = jax.vjp(jax.nn.gelu, pre)
    act = act_full.astype(jnp.bfloat16)
    partial_out = jnp.dot(act, w_down, preferred_element_type=jnp.float32)
    mixed = lax.psum_scatter(partial_out, "tensor", scatter_dimension=1, tiled=True)
    out = (
        (half_x.reshape(count, -1).astype(jnp.float32) + mixed)
        .astype(jnp.bfloat16)
        .reshape(half_x.shape)
    )
    back = jnp.einsum("md,fd->mf", scaled, w_down, preferred_element_type=jnp.float32)
    grad_pre = gelu_back(back)[0].astype(jnp.bfloat16)
    grad_up = jnp.einsum("md,mf->df", flat, grad_pre, preferred_element_type=jnp.float32)
    grad_down_t = jnp.einsum("md,mf->df", scaled, act, preferred_element_type=jnp.float32)
    return (out, grad_up, grad_down_t)


def local(
    ref_image,
    ref_text,
    learner_image,
    learner_text,
    patches,
    cotangent,
    w_up,
    w_down,
    counts,
    sel_index,
    sel_dest,
):
    group_at = lax.axis_index("group")
    mine = lax.cond(
        group_at == 0,
        lambda: pair_losses(ref_image, ref_text, 10.0, -5.0),
        lambda: pair_losses(learner_image, learner_text, 10.0, -5.0),
    )
    partner = partner_2(mine, "group", 0)
    learner_loss = jnp.where(group_at == 1, mine, partner)
    reference_loss = jnp.where(group_at == 0, mine, partner)
    learnability = learner_loss - reference_loss
    shard_scores = lax.all_gather(learnability, "tensor", axis=0, tiled=True)
    n_dp = lax.axis_size("dp")
    slots = sel_index.shape[0]
    cap = max(2, 2 * slots // n_dp)
    patch_rows, half_width = (patches.shape[1], patches.shape[2])
    live = jnp.arange(slots, dtype=jnp.int32) < counts[0]
    target = sel_dest[:, 0]
    hits = ((target[:, None] == jnp.arange(n_dp, dtype=jnp.int32)[None, :]) & live[:, None]).astype(
        jnp.int32
    )
    rank = jnp.sum((jnp.cumsum(hits, axis=0) - hits) * hits, axis=1)
    bucket = target * cap + rank
    placer = (
        (jnp.arange(n_dp * cap, dtype=jnp.int32)[:, None] == bucket[None, :]) & live[None, :]
    ).astype(jnp.bfloat16)
    picked = sel_index[:, None] == jnp.arange(patches.shape[0], dtype=jnp.int32)[None, :]
    score_sel = jnp.sum(jnp.where(picked, shard_scores[None, :], 0.0), axis=1)
    weight = jnp.where(live, jax.nn.sigmoid(score_sel), 0.0)
    chosen_x = patches[sel_index]
    chosen_scaled = (weight[:, None, None] * cotangent[sel_index].astype(jnp.float32)).astype(
        jnp.bfloat16
    )
    boxed_x = jnp.dot(
        placer, chosen_x.reshape(slots, -1), preferred_element_type=jnp.float32
    ).astype(jnp.bfloat16)
    boxed_scaled = jnp.dot(
        placer, chosen_scaled.reshape(slots, -1), preferred_element_type=jnp.float32
    ).astype(jnp.bfloat16)
    boxed_x = boxed_x.reshape(n_dp, cap, patch_rows, half_width)
    boxed_scaled = boxed_scaled.reshape(n_dp, cap, patch_rows, half_width)
    recv_x, recv_scaled = (
        lax.all_to_all(boxed_x, "dp", split_axis=0, concat_axis=0, tiled=True),
        lax.all_to_all(boxed_scaled, "dp", split_axis=0, concat_axis=0, tiled=True),
    )
    recv_x = recv_x.reshape(n_dp * cap, patch_rows, half_width)
    recv_scaled = recv_scaled.reshape(n_dp * cap, patch_rows, half_width)
    wide_x, wide_scaled = widen(recv_x, recv_scaled)
    routed, grad_up, grad_down_t = layer(wide_x, wide_scaled, recv_x, w_up, w_down)
    grad_up, grad_down_t = (
        lax.psum_scatter(grad_up, ("dp", "group"), scatter_dimension=0, tiled=True),
        lax.psum_scatter(grad_down_t, ("dp", "group"), scatter_dimension=0, tiled=True),
    )
    return (learnability, routed, grad_up, grad_down_t)


def solution(mesh):
    placed = (
        P(("dp", "tensor"), None),
        P(("dp", "tensor"), None),
        P(("dp", "tensor"), None),
        P(("dp", "tensor"), None),
        P("dp", "group", "tensor"),
        P("dp", "group", "tensor"),
        P(None, "tensor"),
        P("tensor", None),
        P("dp"),
        P("dp"),
        P("dp", None),
    )
    return jax.shard_map(
        local,
        mesh=mesh,
        in_specs=placed,
        out_specs=(
            P(("dp", "tensor")),
            P("dp", "group", "tensor"),
            P(("dp", "group"), "tensor"),
            P(("dp", "group"), "tensor"),
        ),
        check_vma=False,
    )
```

profile of v0, /device:TPU:0, one launch (start us, length us, event | category | flops | bytes accessed | tf_op | source)
XLA Modules:
  0.0 559.4 jit_solution(10657952456172341593)
XLA Ops:
  8.0 0.7 compare_select_fusion.8
  8.8 0.5 copy-done
  9.2 0.6 gather_fusion
  9.8 0.2 copy.19
  10.7 0.7 fusion.49
  11.4 0.1 reduce_window_sum.11
  11.5 0.8 select_reduce_fusion.1
  12.4 0.7 multiply_add_fusion
  13.0 0.4 convolution_convert_fusion.1
  13.5 1.4 copy.20
  14.8 7.3 %all-to-all-start = ((bf16[8,16,8,512]{3,2,1,0:T(8,128)(2,1)}), bf16[8,16,8,512]{3,2,1,0:T(8,128)(2,1)S(1)}, u32[]{:S(2)}, u32[]{:S(2)}) async-start(bf16[8,16,8,512]{3,2,1,0:T(8,128)(2,1)} %bitcast.14), calls=%async_computation | async-start | bytes 2097152 | tf_op jit(solution)/shard_map/all_to_all | solution.py:131
  22.1 96.4 %conditional.1 = (f32[64]{0:T(128)S(1)}) conditional(s32[]{:T(128)} %convert_element_type.63, (bf16[64,1024]{1,0:T(8,128)(2,1)}, bf16[64,1024]{1,0:T(8,128)(2,1)}) %tuple.14, (bf16[64,768]{1,0:T(8,128)(2,1)}, bf16[64,768]{1,0:T(8,128)(2,1)}) %tuple.15), branch_computations={%region_0.5_spmd, %region_5.10_spmd} | conditional | flops 271581248 | bytes 18616512 | solution.py:91
  22.1 0.0 all-gather.11.cloned.1.call-start
  22.2 1.0 fusion.18
  23.2 1.6 fusion.19
  24.9 0.0 all-gather.13.cloned.1.call-start
  24.9 1.0 fusion.16
  25.9 1.6 fusion.17
  27.6 45.5 %all-gather.11.cloned.1.call-done = bf16[1024,768]{1,0:T(8,128)(2,1)} async-done(((bf16[64,768]{1,0:T(8,128)(2,1)}), bf16[1024,768]{1,0:T(8,128)(2,1)}) %all-gather.11.cloned.1.call-update) | async-done | bytes 1572880 | tf_op jit(solution)/shard_map/cond/branch_1_fun/all_gather | solution.py:31
  73.1 2.4 fusion.13
  75.5 40.6 %all-gather.13.cloned.1.call-done = bf16[1024,768]{1,0:T(8,128)(2,1)} async-done(((bf16[64,768]{1,0:T(8,128)(2,1)}), bf16[1024,768]{1,0:T(8,128)(2,1)}) %all-gather.13.cloned.1.call-update) | async-done | bytes 1572880 | tf_op jit(solution)/shard_map/cond/branch_1_fun/all_gather | solution.py:30
  116.1 2.4 fusion.15
  118.5 0.0 all-gather.15.cloned.1.call-start
  118.5 3.1 collective-permute-start
  121.6 1.4 gather_fusion.1
  123.0 1.2 copy.21
  124.3 0.6 dynamic-slice
  125.5 0.5 fusion.60
  126.1 2.4 all-reduce
  128.5 0.2 select_reduce_fusion
  128.7 1.0 copy-done.1
  129.7 0.0 all-gather.17.cloned.1.call-start
  129.8 0.5 convolution_convert_fusion
  130.3 0.4 copy.22
  130.7 29.4 %all_to_all.10 = bf16[8,16,8,512]{3,2,1,0:T(8,128)(2,1)} all-to-all(bf16[8,16,8,512]{3,2,1,0:T(8,128)(2,1)S(1)} %bitcast.55), channel_id=1, replica_groups=mesh['dp'=8,'tensor'=2,'group'=2] {'dp'}, dimensions={0} | all-to-all | bytes 2097152 | tf_op jit(solution)/shard_map/all_to_all | solution.py:132
  160.1 0.0 reduce-scatter.4.cloned.1.call-start
  160.2 7.1 %fusion.39 = f32[1024,2048]{1,0:T(8,128)S(1)} fusion(bf16[1024,2048]{1,0:T(8,128)(2,1)} %param.19, bf16[128,8,1024]{2,1,0:T(8,128)(2,1)} %all-gather.15.cloned.1.call-done), kind=kOutput, calls=%fused_computation.76 | convolution fusion | flops 4294967296 | bytes 14680064 | tf_op jit(solution)/shard_map/dot_general | solution.py:60
  167.3 3.2 copy-done.9
  170.5 6.7 %fusion.59 = f32[1024,1024]{1,0:T(8,128)} fusion(bf16[2048,1024]{1,0:T(8,128)(2,1)S(1)} %copy-done.4, f32[1024,2048]{1,0:T(8,128)S(1)} %fusion.39), kind=kOutput, calls=%fused_computation.107 | convolution fusion | flops 4313841664 | bytes 16777216 | tf_op jit(solution)/shard_map/dot_general | solution.py:63
  177.2 0.2 reduce-scatter.6.cloned.1.call-start
  177.5 16.9 %fusion.27 = f32[1024,2048]{1,0:T(8,128)} fusion(f32[1024,2048]{1,0:T(8,128)} %copy-done.9, bf16[2048,1024]{1,0:T(8,128)(2,1)} %param.20, bf16[128,8,1024]{2,1,0:T(8,128)(2,1)} %all-gather.17.cloned.1.call-done, bf16[128,8,1024]{2,1,0:T(8,128)(2,1)S(1)} %copy-done.5), kind=kOutput, calls=%fused_computation.68 | convolution fusion | flops 8631877632 | bytes 25165824 | tf_op jit(solution)/shard_map/md,mf->df/dot_general | solution.py:72
  194.4 0.0 reduce-scatter.8.cloned.1.call-start
  194.5 1.5 copy-done.6
  196.0 11.7 %fusion.30 = f32[1024,2048]{1,0:T(8,128)} fusion(bf16[128,8,1024]{2,1,0:T(8,128)(2,1)S(1)} %copy-done.6, f32[1024,2048]{1,0:T(8,128)} %copy-done.9), kind=kOutput, calls=%fused_computation.71 | convolution fusion | flops 4313841664 | bytes 18874368 | tf_op jit(solution)/shard_map/md,mf->df/dot_general | solution.py:73
  207.7 1.2 copy-done.2
  208.9 2.9 fusion.41
  211.8 159.5 %reduce-scatter.6.cloned.1.call-done = f32[64,2048]{1,0:T(8,128)} async-done(((f32[1024,2048]{1,0:T(8,128)}), f32[64,2048]{1,0:T(8,128)}) %reduce-scatter.6.cloned.1.call-update) | async-done | bytes 524304 | tf_op jit(solution)/shard_map/reduce_scatter | solution.py:139
  371.3 180.5 %reduce-scatter.8.cloned.1.call-done = f32[64,2048]{1,0:T(8,128)} async-done(((f32[1024,2048]{1,0:T(8,128)}), f32[64,2048]{1,0:T(8,128)}) %reduce-scatter.8.cloned.1.call-update) | async-done | bytes 524304 | tf_op jit(solution)/shard_map/reduce_scatter | solution.py:140
  (35 shorter events, 0.3 us)
Async XLA Ops:
  8.0 1.2 copy-start
  13.5 108.2 %copy-start.3 = (bf16[128,8,512]{2,1,0:T(8,128)(2,1)S(1)}, bf16[128,8,512]{2,1,0:T(8,128)(2,1)}, u32[]{:S(2)}) copy-start(bf16[128,8,512]{2,1,0:T(8,128)(2,1)} %param.18) | copy-start | bytes 3145732
  14.8 113.9 %all-to-all-start = ((bf16[8,16,8,512]{3,2,1,0:T(8,128)(2,1)}), bf16[8,16,8,512]{3,2,1,0:T(8,128)(2,1)S(1)}, u32[]{:S(2)}, u32[]{:S(2)}) async-start(bf16[8,16,8,512]{3,2,1,0:T(8,128)(2,1)} %bitcast.14), calls=%async_computation | async-start | bytes 2097152 | tf_op jit(solution)/shard_map/all_to_all | solution.py:131
  22.1 102.2 %copy-start.8 = (u32[32]{0:T(128)S(1)}, u32[32]{0:T(128)}, u32[]{:S(2)}) copy-start(u32[32]{0:T(128)} %constant.92) | copy-start | bytes 388
  22.1 106.4 %copy-start.7 = (s32[64]{0:T(128)S(1)}, s32[64]{0:T(128)}, u32[]{:S(2)}) copy-start(s32[64]{0:T(128)} %param.22) | copy-start | bytes 772
  22.1 51.0 %all-gather.11.cloned.1.call-start = ((), (), s32[]{:S(2)}) async-start(), calls=%async_computation.7 | async-start | bytes 1671168 | tf_op jit(solution)/shard_map/cond/branch_1_fun/all_gather | solution.py:31
  24.9 91.2 %all-gather.13.cloned.1.call-start = ((), (), s32[]{:S(2)}) async-start(), calls=%async_computation.8 | async-start | bytes 1671168 | tf_op jit(solution)/shard_map/cond/branch_1_fun/all_gather | solution.py:30
  118.5 41.7 %all-gather.15.cloned.1.call-start = ((), (), s32[]{:S(2)}) async-start(), calls=%async_computation.9 | async-start | bytes 3145728 | tf_op jit(solution)/shard_map/all_gather | solution.py:50
  118.5 7.0 %collective-permute-start = (f32[64]{0:T(128)S(1)}, f32[64]{0:T(128)S(1)}, u32[]{:S(2)}, u32[]{:S(2)}) collective-permute-start(f32[64]{0:T(128)S(1)} %get-tuple-element.29), channel_id=1, source_target_pairs={{0,1},{1,0},{2,3},{3,2},{4,5},{5,4},{6,7},{7,6},{8,9},{9,8},{10,11... | collective-permute-start | bytes 776 | tf_op jit(solution)/shard_map/ppermute | solution.py:14
  128.7 1.0 copy-start.1
  129.7 47.8 %all-gather.17.cloned.1.call-start = ((), (), s32[]{:S(2)}) async-start(), calls=%async_computation.11 | async-start | bytes 3145728 | tf_op jit(solution)/shard_map/all_gather | solution.py:51
  160.1 47.6 %reduce-scatter.4.cloned.1.call-start = ((), (), s32[]{:S(2)}) async-start(), calls=%async_computation.10 | async-start | bytes 6291456 | tf_op jit(solution)/shard_map/reduce_scatter | solution.py:64
  160.2 10.3 %copy-start.4 = (bf16[2048,1024]{1,0:T(8,128)(2,1)S(1)}, bf16[2048,1024]{1,0:T(8,128)(2,1)}, u32[]{:S(2)}) copy-start(bf16[2048,1024]{1,0:T(8,128)(2,1)} %param.20) | copy-start | bytes 12582916
  167.3 3.2 copy-start.9
  170.5 7.0 %copy-start.5 = (bf16[128,8,1024]{2,1,0:T(8,128)(2,1)S(1)}, bf16[128,8,1024]{2,1,0:T(8,128)(2,1)}, u32[]{:S(2)}) copy-start(bf16[128,8,1024]{2,1,0:T(8,128)(2,1)} %all-gather.15.cloned.1.call-done) | copy-start | bytes 6291460
  177.2 194.1 %reduce-scatter.6.cloned.1.call-start = ((), (), s32[]{:S(2)}) async-start(), calls=%async_computation.12 | async-start | bytes 8912896 | tf_op jit(solution)/shard_map/reduce_scatter | solution.py:139
  194.4 1.6 copy-start.6
  194.4 357.4 %reduce-scatter.8.cloned.1.call-start = ((), (), s32[]{:S(2)}) async-start(), calls=%async_computation.13 | async-start | bytes 8912896 | tf_op jit(solution)/shard_map/reduce_scatter | solution.py:140
  207.7 1.2 copy-start.2
Sparse Core Ops, SparseCore 0:
  25.8 47.2 all-gather.10
  76.0 40.0 all-gather.12
Sparse Core Ops, SparseCore 1:
  129.8 8.3 all-gather.14
  160.2 8.6 all-gather.16
  177.3 10.3 reduce-scatter.3
  194.5 176.7 reduce-scatter.5
  374.3 177.5 reduce-scatter.7
where the time goes:
time: 560 us; the launch traced here: 559 us
  waiting for transfers between devices  426 us (76%)
  matrix products  48 us (9%)
  blocking collectives  31.9 us (6%)
  between operations  17.2 us (3%)
  local copies, waits for them, and re-layouts  13.1 us (2%)
  other arithmetic  12 us (2%)
  starting transfers between devices  10.8 us (2%)
    reduce_scatter x1, waiting for transfers between devices, local(): lax.psum_scatter(grad_down_t, ('dp', 'group'), scatter_dimension=0, tiled...  181 us
    reduce_scatter x1, waiting for transfers between devices, local(): lax.psum_scatter(grad_up, ('dp', 'group'), scatter_dimension=0, tiled=True)  159 us
    all_gather x1, waiting for transfers between devices, pair_losses(): far_txt = lax.all_gather(unit_txt, ('dp', 'tensor'), axis=0, tiled=True)  45.5 us
    all_gather x1, waiting for transfers between devices, pair_losses(): far_img = lax.all_gather(unit_img, ('dp', 'tensor'), axis=0, tiled=True)  40.6 us
    all_to_all x1, blocking collectives, local(): lax.all_to_all(boxed_scaled, 'dp', split_axis=0, concat_axis=0, tiled=True)  29.4 us
    dot_general x1, matrix products, layer(): jnp.einsum('md,mf->df', flat, grad_pre, preferred_element_type=jnp.float32)  16.9 us
    dot_general x1, matrix products, layer(): jnp.einsum('md,mf->df', scaled, act, preferred_element_type=jnp.float32)  11.7 us
  transfers between devices with their start and end apart: 9, of which 4 were waited for; matrix products, arithmetic and copies ran while one was open for 11% of the time, Pallas kernels for 0%

commit v1 on v0

v1 whole, which is shorter than its diff:
```python
import jax
import jax.numpy as jnp
from jax import lax
from jax.sharding import PartitionSpec as P


def swap(block, axes, mask):
    names = tuple(axes)
    sizes = [lax.axis_size(name) for name in names]
    total = 1
    for size in sizes:
        total *= size
    route = []
    for start in range(total):
        rest, end, scale = start, 0, 1
        for size, bits in zip(reversed(sizes), reversed(mask)):
            end += ((rest % size) ^ bits) * scale
            rest //= size
            scale *= size
        route.append((start, end))
    return lax.ppermute(block, names if len(names) > 1 else names[0], route)


def unit_rows(block):
    wide = block.astype(jnp.float32)
    return (wide * lax.rsqrt(jnp.sum(wide * wide, axis=1, keepdims=True) + 1e-06)).astype(
        jnp.bfloat16
    )


def loss_parts(image, text, temp, bias):
    rows = image.shape[0]
    far = lax.axis_size("dp") // 2
    near_masks = [(0, 0), (0, 1), (1, 0), (1, 1)]
    images = [image] + [swap(image, ("dp", "tensor"), mask) for mask in near_masks[1:]]
    texts = [text] + [swap(text, ("dp",), (2 * mask,)) for mask in range(1, far)]
    img = jnp.concatenate(images, axis=0)
    txt = jnp.concatenate(texts, axis=0)
    scores = temp * jnp.einsum("rd,kd->rk", img, txt, preferred_element_type=jnp.float32) + bias
    at_row = jnp.arange(img.shape[0], dtype=jnp.int32)[:, None]
    at_col = jnp.arange(txt.shape[0], dtype=jnp.int32)[None, :]
    same = (at_row == at_col) & (at_row < rows)
    terms = jax.nn.softplus(jnp.where(same, -scores, scores))
    by_image = jnp.sum(terms, axis=1).reshape(2, 2, rows)
    by_text = jnp.sum(terms, axis=0).reshape(far, rows)
    of_shard = by_image[0] + swap(by_image[1], ("dp",), (1,))
    of_text = by_text[0]
    for mask in range(1, far):
        of_text = of_text + swap(by_text[mask], ("dp",), (2 * mask,))
    return 0.5 * jnp.stack([of_shard[0] + of_text, of_shard[1]])


def scatter_sum(block, order, axis_bits):
    bits = len(axis_bits)
    width = block.shape[1]
    cut = block.reshape((2,) * bits + (-1, width))
    left = list(range(bits))
    for step, bit in enumerate(order):
        name, mask = axis_bits[bit]
        mine = (lax.axis_index(name) // mask) % 2
        at = left.index(bit)
        left.remove(bit)
        keep = lax.dynamic_index_in_dim(cut, mine, at, keepdims=False)
        send = lax.dynamic_index_in_dim(cut, 1 - mine, at, keepdims=False)
        came = swap(send, (name,), (mask,))
        cut = keep.astype(jnp.float32) + came.astype(jnp.float32)
        if step < bits - 1:
            cut = cut.astype(jnp.bfloat16)
    return cut


def part_orders(bits):
    group, near, next_near = bits - 1, bits - 2, bits - 3
    rest = [bit for bit in range(bits - 4, -1, -1)]
    return [
        [near, group, next_near] + rest,
        [group, near, next_near] + rest,
        [next_near, near, group] + rest,
    ]


def local(
    ref_image,
    ref_text,
    learner_image,
    learner_text,
    patches,
    cotangent,
    w_up,
    w_down,
    counts,
    sel_index,
    sel_dest,
):
    group_at = lax.axis_index("group")
    tensor_at = lax.axis_index("tensor")
    dp_at = lax.axis_index("dp")
    n_dp = lax.axis_size("dp")
    extra = learner_image.shape[1] - ref_image.shape[1]
    is_ref = group_at == 0

    def own_model(ref_block, learner_block):
        ref_block = jnp.pad(ref_block, ((0, 0), (0, extra)))
        return unit_rows(jnp.where(is_ref, ref_block, learner_block))

    share = loss_parts(
        own_model(ref_image, learner_image), own_model(ref_text, learner_text), 10.0, -5.0
    )

    slots = sel_index.shape[0]
    cap = max(2, 2 * slots // n_dp)
    patch_rows, half_width = (patches.shape[1], patches.shape[2])
    count = slots * patch_rows
    half_x = patches[sel_index].reshape(count, half_width)
    half_cot = cotangent[sel_index].reshape(count, half_width)

    def widen(half):
        other = swap(half, ("tensor",), (1,))
        return jnp.concatenate(
            [jnp.where(tensor_at == 0, half, other), jnp.where(tensor_at == 0, other, half)], axis=1
        )

    x = widen(half_x)
    cot = widen(half_cot)
    pre = jnp.dot(x, w_up, preferred_element_type=jnp.float32)
    act_full, gelu_back = jax.vjp(jax.nn.gelu, pre)
    act = lax.optimization_barrier(act_full.astype(jnp.bfloat16))
    partial_out = jnp.dot(act, w_down, preferred_element_type=jnp.float32)
    back = jnp.einsum("md,fd->mf", cot, w_down, preferred_element_type=jnp.float32)
    grad_pre = lax.optimization_barrier(gelu_back(back)[0])

    halves = partial_out.reshape(count, 2, half_width)
    keep = lax.dynamic_index_in_dim(halves, tensor_at, 1, keepdims=False)
    send = lax.dynamic_index_in_dim(halves, 1 - tensor_at, 1, keepdims=False)
    came = swap(send.astype(jnp.bfloat16), ("tensor",), (1,))
    out = (half_x.astype(jnp.float32) + (keep + came.astype(jnp.float32))).astype(jnp.bfloat16)

    live = jnp.arange(slots, dtype=jnp.int32) < counts[0]
    target = sel_dest[:, 0]
    earlier = jnp.arange(slots)[:, None] > jnp.arange(slots)[None, :]
    rank = jnp.sum(
        (earlier & (target[:, None] == target[None, :]) & live[None, :]).astype(jnp.int32), axis=1
    )
    bucket = (target ^ dp_at) * cap + rank
    placer = (
        (jnp.arange(n_dp * cap, dtype=jnp.int32)[:, None] == bucket[None, :]) & live[None, :]
    ).astype(jnp.bfloat16)
    boxed = jnp.dot(
        placer, out.reshape(slots, patch_rows * half_width), preferred_element_type=jnp.float32
    ).astype(jnp.bfloat16)
    boxed = boxed.reshape(n_dp, cap, patch_rows, half_width)
    landed = jnp.stack(
        [boxed[0]] + [swap(boxed[mask], ("dp",), (mask,)) for mask in range(1, n_dp)]
    )
    routed = landed[jnp.arange(n_dp, dtype=jnp.int32) ^ dp_at].reshape(
        n_dp * cap, patch_rows, half_width
    )

    share = jnp.where(tensor_at == 0, share, share[::-1])
    mine = share + swap(share, ("tensor",), (1,))
    partner = swap(share, ("group",), (1,)) + swap(share, ("tensor", "group"), (1, 1))
    shard_scores = jnp.where(is_ref, partner - mine, mine - partner)
    learnability = lax.dynamic_index_in_dim(shard_scores, tensor_at, 0, keepdims=False)
    picked = sel_index[:, None] == jnp.arange(patches.shape[0], dtype=jnp.int32)[None, :]
    score_sel = jnp.sum(jnp.where(picked, shard_scores.reshape(1, -1), 0.0), axis=1)
    weight = jnp.where(live, jax.nn.sigmoid(score_sel), 0.0)
    row_weight = jnp.repeat(weight, patch_rows)[:, None]

    axis_bits = [("dp", 1 << bit) for bit in range(n_dp.bit_length() - 2, -1, -1)] + [("group", 1)]
    hidden = w_up.shape[1]
    edges = [0, hidden * 3 // 8, hidden * 3 // 4, hidden]
    orders = part_orders(len(axis_bits))
    sums = []
    for rows, cols in ((x, grad_pre), (cot, act)):
        scaled = (row_weight * cols.astype(jnp.float32)).astype(jnp.bfloat16)
        parts = []
        for order, low, high in zip(orders, edges[:-1], edges[1:]):
            product = jnp.einsum(
                "md,mf->df", rows, scaled[:, low:high], preferred_element_type=jnp.float32
            ).astype(jnp.bfloat16)
            parts.append(scatter_sum(product, order, axis_bits))
        sums.append(jnp.concatenate(parts, axis=1))
    return (learnability, routed, sums[0], sums[1])


def solution(mesh):
    placed = (
        P(("dp", "tensor"), None),
        P(("dp", "tensor"), None),
        P(("dp", "tensor"), None),
        P(("dp", "tensor"), None),
        P("dp", "group", "tensor"),
        P("dp", "group", "tensor"),
        P(None, "tensor"),
        P("tensor", None),
        P("dp"),
        P("dp"),
        P("dp", None),
    )
    return jax.shard_map(
        local,
        mesh=mesh,
        in_specs=placed,
        out_specs=(
            P(("dp", "tensor")),
            P("dp", "group", "tensor"),
            P(("dp", "group"), "tensor"),
            P(("dp", "group"), "tensor"),
        ),
        check_vma=False,
    )
```

time: 560 us -> 205 us (0.37)
  waiting for transfers between devices: 426 us -> 79.4 us
  starting transfers between devices: 10.8 us -> 58.7 us
  blocking collectives: 31.9 us -> 0 us
  matrix products: 48 us -> 20 us
  between operations: 17.2 us -> 2.35 us
  local copies, waits for them, and re-layouts: 13.1 us -> 24.8 us
  other arithmetic: 12 us -> 18.7 us
    reduce_scatter x3 -> x0, waiting for transfers between devices: 340 us -> none  [the longest x1 181 us: local(): lax.psum_scatter(grad_down_t, ('dp', 'group'), scatter_dimension=0, tiled...]
    all_gather x4 -> x0, waiting for transfers between devices: 86.1 us -> none  [the longest x1 45.5 us: pair_losses(): far_txt = lax.all_gather(unit_txt, ('dp', 'tensor'), axis=0, tiled=True)]
    ppermute x1 -> x47, waiting for transfers between devices: 0.01 us -> 79.4 us  [swap(): return lax.ppermute(block, names if len(names) > 1 else names[0], route)]
    ppermute x1 -> x47, starting transfers between devices: 3.1 us -> 58.7 us  [swap(): return lax.ppermute(block, names if len(names) > 1 else names[0], route)]
    all_to_all x1 -> x0, blocking collectives: 29.4 us -> none  [local(): lax.all_to_all(boxed_scaled, 'dp', split_axis=0, concat_axis=0, tiled=True)]
    dot_general x8 -> x11, matrix products: 48 us -> 20 us  [the longest x6 6.78 us: local(): jnp.einsum('md,mf->df', rows, scaled[:, low:high], preferred_element_type...]
    dynamic_slice x0 -> x14, local copies, waits for them, and re-layouts: none -> 12.3 us  [the longest x6 5.5 us: scatter_sum(): send = lax.dynamic_index_in_dim(cut, 1 - mine, at, keepdims=False)]
    convert_element_type x1 -> x20, other arithmetic: 0.73 us -> 10.1 us  [the longest x18 8.52 us: scatter_sum(): cut = cut.astype(jnp.bfloat16)]
  transfers between devices with their start and end apart: 9 -> 47, of which waited for: 4 -> 24; matrix products, arithmetic and copies ran while one was open for 11% -> 19% of each run, Pallas kernels for 0% -> 0%
where the time goes in v1:
time: 205 us; the launch traced here: 204 us
  waiting for transfers between devices  79.4 us (39%)
  starting transfers between devices  58.7 us (29%)
  local copies, waits for them, and re-layouts  24.8 us (12%)
  matrix products  20 us (10%)
  other arithmetic  18.7 us (9%)
  between operations  2.35 us (1%)
    ppermute x47, waiting for transfers between devices, swap(): return lax.ppermute(block, names if len(names) > 1 else names[0], route)  79.4 us
    ppermute x47, starting transfers between devices, swap(): return lax.ppermute(block, names if len(names) > 1 else names[0], route)  58.7 us
    convert_element_type x18, other arithmetic, scatter_sum(): cut = cut.astype(jnp.bfloat16)  8.52 us
    dot_general x6, matrix products, local(): jnp.einsum('md,mf->df', rows, scaled[:, low:high], preferred_element_type...  6.78 us
    dynamic_slice x6, local copies, waits for them, and re-layouts, scatter_sum(): send = lax.dynamic_index_in_dim(cut, 1 - mine, at, keepdims=False)  5.5 us
    dynamic_slice x6, local copies, waits for them, and re-layouts, scatter_sum(): keep = lax.dynamic_index_in_dim(cut, mine, at, keepdims=False)  4.92 us
    dot_general x1, matrix products, local(): jnp.einsum('md,fd->mf', cot, w_down, preferred_element_type=jnp.float32)  4.44 us
  transfers between devices with their start and end apart: 47, of which 24 were waited for; matrix products, arithmetic and copies ran while one was open for 19% of the time, Pallas kernels for 0%

profile of v1, /device:TPU:0, one launch (start us, length us, event | category | flops | bytes accessed | tf_op | source)
XLA Modules:
  0.0 204.0 jit_solution(1074431409892063505)
XLA Ops:
  3.4 2.6 %collective-permute-start.1 = (bf16[64,1024]{1,0:T(8,128)(2,1)S(1)}, bf16[64,1024]{1,0:T(8,128)(2,1)S(1)}, u32[]{:S(2)}, u32[]{:S(2)}) collective-permute-start(bf16[64,1024]{1,0:T(8,128)(2,1)S(1)} %fusion.51), channel_id=1, source_target_pairs={{0,4},{2,6},{4,0},{6,2},{8,12},{10,14},{12,8},{14,10},{16,20},{18,... | collective-permute-start | bytes 393224 | tf_op jit(solution)/shard_map/ppermute | solution.py:21
  8.1 1.9 collective-permute-start.3
  9.9 2.6 %collective-permute-start.4 = (bf16[64,1024]{1,0:T(8,128)(2,1)S(1)}, bf16[64,1024]{1,0:T(8,128)(2,1)}, u32[]{:S(2)}, u32[]{:S(2)}) collective-permute-start(bf16[64,1024]{1,0:T(8,128)(2,1)S(1)} %fusion.53), channel_id=1, source_target_pairs={{0,16},{4,20},{8,24},{12,28},{16,0},{20,4},{24,8},{28,12},{1,17},{... | collective-permute-start | bytes 393224 | tf_op jit(solution)/shard_map/ppermute | solution.py:21
  17.0 2.3 %collective-permute-done.4 = bf16[64,1024]{1,0:T(8,128)(2,1)} collective-permute-done((bf16[64,1024]{1,0:T(8,128)(2,1)S(1)}, bf16[64,1024]{1,0:T(8,128)(2,1)}, u32[]{:S(2)}, u32[]{:S(2)}) %collective-permute-start.4) | collective-permute-done | bytes 131104 | tf_op jit(solution)/shard_map/ppermute | solution.py:21
  19.3 3.4 %collective-permute-done.5 = bf16[64,1024]{1,0:T(8,128)(2,1)} collective-permute-done((bf16[64,1024]{1,0:T(8,128)(2,1)S(1)}, bf16[64,1024]{1,0:T(8,128)(2,1)}, u32[]{:S(2)}, u32[]{:S(2)}) %collective-permute-start.5) | collective-permute-done | bytes 131104 | tf_op jit(solution)/shard_map/ppermute | solution.py:21
  22.7 1.5 fusion.73
  24.3 1.5 collective-permute-start.6
  26.0 2.7 %collective-permute-start.7 = (f32[64]{0:T(128)S(1)}, f32[64]{0:T(128)S(1)}, u32[]{:S(2)}, u32[]{:S(2)}) collective-permute-start(f32[64]{0:T(128)S(1)} %get-tuple-element.32), channel_id=1, source_target_pairs={{0,8},{4,12},{8,0},{12,4},{16,24},{20,28},{24,16},{28,20},{1,9},{5... | collective-permute-start | bytes 776 | tf_op jit(solution)/shard_map/ppermute | solution.py:21
  31.2 1.9 collective-permute-done.8
  33.2 1.9 collective-permute-done.9
  35.1 1.8 collective-permute-start.10
  41.2 2.4 %copy-done.17 = bf16[1024,2048]{1,0:T(8,128)(2,1)S(1)} copy-done((bf16[1024,2048]{1,0:T(8,128)(2,1)S(1)}, bf16[1024,2048]{1,0:T(8,128)(2,1)}, u32[]{:S(2)}) %copy-start.17) | copy-done | bytes 4194328
  43.5 3.2 %multiply_convert_fusion.2 = (bf16[512,2048]{1,0:T(8,128)(2,1)S(1)}, f32[512,2048]{1,0:T(8,128)S(1)}) fusion(bf16[1024,2048]{1,0:T(8,128)(2,1)S(1)} %copy-done.17, bf16[512,512]{1,0:T(8,128)(2,1)S(1)} %get-tuple-element.39, bf16[512,512]{1,0:T(8,128)(2,1)S(1)} %get-tuple-element.40), kind=kOutput, calls=%fused_computation.14 | convolution fusion | flops 2159017984 | bytes 11534336 | tf_op jit(solution)/shard_map/dot_general | solution.py:125
  46.7 4.4 %fusion.5 = f32[512,2048]{1,0:T(8,128)S(1)} fusion(f32[512,2048]{1,0:T(8,128)S(1)} %get-tuple-element.38, bf16[2048,1024]{1,0:T(8,128)(2,1)S(1)} %copy-done.18, bf16[512,512]{1,0:T(8,128)(2,1)S(1)} %get-tuple-element.19, bf16[512,512]{1,0:T(8,128)(2,1)S(1)} %get-tuple-element.18), kind=kOutput, calls=%fused_computation.11 | convolution fusion | flops 2169503744 | bytes 13631488 | tf_op jit(solution)/shard_map/md,fd->mf/dot_general | solution.py:129
  57.5 3.7 %fusion.77 = f32[512,1024]{1,0:T(8,128)} fusion(bf16[512,2048]{1,0:T(8,128)(2,1)S(1)} %get-tuple-element.37, bf16[2048,1024]{1,0:T(8,128)(2,1)S(1)} %copy-done.18), kind=kOutput, calls=%fused_computation.199 | convolution fusion | flops 2147483648 | bytes 8388608 | tf_op jit(solution)/shard_map/dot_general | solution.py:128
  70.2 1.5 collective-permute-start.23
  72.7 3.0 %reshape.188 = f32[512,2,512]{2,1,0:T(2,128)S(1)} reshape(f32[512,1024]{1,0:T(8,128)} %fusion.77) | data formatting | bytes 4194304 | tf_op jit(solution)/shard_map/reshape | solution.py:132
  77.0 1.8 convolution_convert_fusion.6
  81.4 1.9 collective-permute-start.31
  84.5 1.5 collective-permute-start.27
  88.0 8.1 %collective-permute-done.31 = bf16[2,2,2,64,512]{4,3,0,2,1:T(8,128)(2,1)S(1)} collective-permute-done((bf16[2,2,2,64,512]{4,3,0,2,1:T(8,128)(2,1)}, bf16[2,2,2,64,512]{4,3,0,2,1:T(8,128)(2,1)S(1)}, u32[]{:S(2)}, u32[]{:S(2)}) %collective-permute-start.31) | collective-permute-done | bytes 524320 | tf_op jit(solution)/shard_map/ppermute | solution.py:21
  98.3 3.2 %collective-permute-done.15 = bf16[16,8,512]{2,1,0:T(8,128)(2,1)S(1)} collective-permute-done((bf16[16,8,512]{2,1,0:T(8,128)(2,1)S(1)}, bf16[16,8,512]{2,1,0:T(8,128)(2,1)S(1)}, u32[]{:S(2)}, u32[]{:S(2)}) %collective-permute-start.15) | collective-permute-done | bytes 131104 | tf_op jit(solution)/shard_map/ppermute | solution.py:21
  101.4 1.6 collective-permute-start.16
  103.0 3.4 %collective-permute-done.16 = bf16[16,8,512]{2,1,0:T(8,128)(2,1)S(1)} collective-permute-done((bf16[16,8,512]{2,1,0:T(8,128)(2,1)S(1)}, bf16[16,8,512]{2,1,0:T(8,128)(2,1)S(1)}, u32[]{:S(2)}, u32[]{:S(2)}) %collective-permute-start.16) | collective-permute-done | bytes 131104 | tf_op jit(solution)/shard_map/ppermute | solution.py:21
  106.4 1.5 collective-permute-start.17
  108.0 4.3 %collective-permute-done.17 = bf16[16,8,512]{2,1,0:T(8,128)(2,1)S(1)} collective-permute-done((bf16[16,8,512]{2,1,0:T(8,128)(2,1)S(1)}, bf16[16,8,512]{2,1,0:T(8,128)(2,1)S(1)}, u32[]{:S(2)}, u32[]{:S(2)}) %collective-permute-start.17) | collective-permute-done | bytes 131104 | tf_op jit(solution)/shard_map/ppermute | solution.py:21
  112.3 1.6 collective-permute-start.18
  113.8 4.3 %collective-permute-done.18 = bf16[16,8,512]{2,1,0:T(8,128)(2,1)S(1)} collective-permute-done((bf16[16,8,512]{2,1,0:T(8,128)(2,1)S(1)}, bf16[16,8,512]{2,1,0:T(8,128)(2,1)S(1)}, u32[]{:S(2)}, u32[]{:S(2)}) %collective-permute-start.18) | collective-permute-done | bytes 131104 | tf_op jit(solution)/shard_map/ppermute | solution.py:21
  118.1 2.4 %collective-permute-start.19 = (bf16[16,8,512]{2,1,0:T(8,128)(2,1)S(1)}, bf16[16,8,512]{2,1,0:T(8,128)(2,1)S(1)}, u32[]{:S(2)}, u32[]{:S(2)}) collective-permute-start(bf16[16,8,512]{2,1,0:T(8,128)(2,1)S(1)} %bitcast.235), channel_id=1, source_target_pairs={{0,20},{4,16},{8,28},{12,24},{16,4},{20,0},{24,12},{28,8},{1,21},{... | collective-permute-start | bytes 393224 | tf_op jit(solution)/shard_map/ppermute | solution.py:21
  120.6 5.0 %collective-permute-done.19 = bf16[16,8,512]{2,1,0:T(8,128)(2,1)S(1)} collective-permute-done((bf16[16,8,512]{2,1,0:T(8,128)(2,1)S(1)}, bf16[16,8,512]{2,1,0:T(8,128)(2,1)S(1)}, u32[]{:S(2)}, u32[]{:S(2)}) %collective-permute-start.19) | collective-permute-done | bytes 131104 | tf_op jit(solution)/shard_map/ppermute | solution.py:21
  125.5 5.9 %collective-permute-start.20 = (bf16[16,8,512]{2,1,0:T(8,128)(2,1)S(1)}, bf16[16,8,512]{2,1,0:T(8,128)(2,1)S(1)}, u32[]{:S(2)}, u32[]{:S(2)}) collective-permute-start(bf16[16,8,512]{2,1,0:T(8,128)(2,1)S(1)} %bitcast.234), channel_id=1, source_target_pairs={{0,24},{4,28},{8,16},{12,20},{16,8},{20,12},{24,0},{28,4},{1,25},{... | collective-permute-start | bytes 393224 | tf_op jit(solution)/shard_map/ppermute | solution.py:21
  131.5 3.6 %collective-permute-done.20 = bf16[16,8,512]{2,1,0:T(8,128)(2,1)S(1)} collective-permute-done((bf16[16,8,512]{2,1,0:T(8,128)(2,1)S(1)}, bf16[16,8,512]{2,1,0:T(8,128)(2,1)S(1)}, u32[]{:S(2)}, u32[]{:S(2)}) %collective-permute-start.20) | collective-permute-done | bytes 131104 | tf_op jit(solution)/shard_map/ppermute | solution.py:21
  135.1 3.9 %collective-permute-start.21 = (bf16[16,8,512]{2,1,0:T(8,128)(2,1)S(1)}, bf16[16,8,512]{2,1,0:T(8,128)(2,1)S(1)}, u32[]{:S(2)}, u32[]{:S(2)}) collective-permute-start(bf16[16,8,512]{2,1,0:T(8,128)(2,1)S(1)} %bitcast.233), channel_id=1, source_target_pairs={{0,28},{4,24},{8,20},{12,16},{16,12},{20,8},{24,4},{28,0},{1,29},{... | collective-permute-start | bytes 393224 | tf_op jit(solution)/shard_map/ppermute | solution.py:21
  139.0 4.0 %collective-permute-done.21 = bf16[16,8,512]{2,1,0:T(8,128)(2,1)S(1)} collective-permute-done((bf16[16,8,512]{2,1,0:T(8,128)(2,1)S(1)}, bf16[16,8,512]{2,1,0:T(8,128)(2,1)S(1)}, u32[]{:S(2)}, u32[]{:S(2)}) %collective-permute-start.21) | collective-permute-done | bytes 131104 | tf_op jit(solution)/shard_map/ppermute | solution.py:21
  142.9 2.2 %collective-permute-start.44 = (bf16[2,2,64,512]{3,2,0,1:T(8,128)(2,1)}, bf16[2,2,64,512]{3,2,0,1:T(8,128)(2,1)}, u32[]{:S(2)}, u32[]{:S(2)}) collective-permute-start(bf16[2,2,64,512]{3,2,0,1:T(8,128)(2,1)} %dynamic-slice_bitcast_fusion.4), channel_id=1, source_target_pairs={{0,4},{4,0},{8,12},{12,8},{16,20},{20,16},{24,28},{28,24},{1,5},{5... | collective-permute-start | bytes 786440 | tf_op jit(solution)/shard_map/ppermute | solution.py:21
  145.1 1.6 gather_fusion.1
  148.2 3.8 %collective-permute-start.36 = (bf16[2,2,64,768]{3,2,0,1:T(8,128)(2,1)S(1)}, bf16[2,2,64,768]{3,2,0,1:T(8,128)(2,1)S(1)}, u32[]{:S(2)}, u32[]{:S(2)}) collective-permute-start(bf16[2,2,64,768]{3,2,0,1:T(8,128)(2,1)S(1)} %dynamic-slice_bitcast_fusion.1), channel_id=1, source_target_pairs={{0,1},{1,0},{2,3},{3,2},{4,5},{5,4},{6,7},{7,6},{8,9},{9,8},{10,11... | collective-permute-start | bytes 1179656 | tf_op jit(solution)/shard_map/ppermute | solution.py:21
  155.7 1.9 collective-permute-start.45
  161.7 1.5 collective-permute-start.33
  163.3 5.0 %collective-permute-done.33 = bf16[2,64,512]{2,1,0:T(8,128)(2,1)S(1)} collective-permute-done((bf16[2,64,512]{2,1,0:T(8,128)(2,1)S(1)}, bf16[2,64,512]{2,1,0:T(8,128)(2,1)S(1)}, u32[]{:S(2)}, u32[]{:S(2)}) %collective-permute-start.33) | collective-permute-done | bytes 131104 | tf_op jit(solution)/shard_map/ppermute | solution.py:21
  168.3 6.2 %collective-permute-done.46 = bf16[64,512]{1,0:T(8,128)(2,1)S(1)} collective-permute-done((bf16[64,512]{1,0:T(8,128)(2,1)S(1)}, bf16[64,512]{1,0:T(8,128)(2,1)S(1)}, u32[]{:S(2)}, u32[]{:S(2)}) %collective-permute-start.46) | collective-permute-done | bytes 65568 | tf_op jit(solution)/shard_map/ppermute | solution.py:21
  174.5 9.6 %collective-permute-done.34 = bf16[64,512]{1,0:T(8,128)(2,1)S(1)} collective-permute-done((bf16[64,512]{1,0:T(8,128)(2,1)S(1)}, bf16[64,512]{1,0:T(8,128)(2,1)S(1)}, u32[]{:S(2)}, u32[]{:S(2)}) %collective-permute-start.34) | collective-permute-done | bytes 65568 | tf_op jit(solution)/shard_map/ppermute | solution.py:21
  184.5 2.1 %collective-permute-start.41 = (bf16[2,64,768]{2,1,0:T(8,128)(2,1)S(1)}, bf16[2,64,768]{2,1,0:T(8,128)(2,1)S(1)}, u32[]{:S(2)}, u32[]{:S(2)}) collective-permute-start(bf16[2,64,768]{2,1,0:T(8,128)(2,1)S(1)} %dynamic-slice_bitcast_fusion.6), channel_id=1, source_target_pairs={{0,8},{4,12},{8,0},{12,4},{16,24},{20,28},{24,16},{28,20},{1,9},{5... | collective-permute-start | bytes 589832 | tf_op jit(solution)/shard_map/ppermute | solution.py:21
  186.9 2.1 %collective-permute-start.29 = (bf16[2,64,768]{2,1,0:T(8,128)(2,1)S(1)}, bf16[2,64,768]{2,1,0:T(8,128)(2,1)S(1)}, u32[]{:S(2)}, u32[]{:S(2)}) collective-permute-start(bf16[2,64,768]{2,1,0:T(8,128)(2,1)S(1)} %dynamic-slice_bitcast_fusion.8), channel_id=1, source_target_pairs={{0,8},{4,12},{8,0},{12,4},{16,24},{20,28},{24,16},{28,20},{1,9},{5... | collective-permute-start | bytes 589832 | tf_op jit(solution)/shard_map/ppermute | solution.py:21
  190.2 1.9 collective-permute-done.41
  195.3 2.0 %collective-permute-done.29 = bf16[2,64,768]{2,1,0:T(8,128)(2,1)S(1)} collective-permute-done((bf16[2,64,768]{2,1,0:T(8,128)(2,1)S(1)}, bf16[2,64,768]{2,1,0:T(8,128)(2,1)S(1)}, u32[]{:S(2)}, u32[]{:S(2)}) %collective-permute-start.29) | collective-permute-done | bytes 196640 | tf_op jit(solution)/shard_map/ppermute | solution.py:21
  197.6 2.3 %collective-permute-done.42 = bf16[64,768]{1,0:T(8,128)(2,1)S(1)} collective-permute-done((bf16[64,768]{1,0:T(8,128)(2,1)S(1)}, bf16[64,768]{1,0:T(8,128)(2,1)S(1)}, u32[]{:S(2)}, u32[]{:S(2)}) %collective-permute-start.42) | collective-permute-done | bytes 98336 | tf_op jit(solution)/shard_map/ppermute | solution.py:21
  201.0 2.1 %collective-permute-done.30 = bf16[64,768]{1,0:T(8,128)(2,1)S(1)} collective-permute-done((bf16[64,768]{1,0:T(8,128)(2,1)S(1)}, bf16[64,768]{1,0:T(8,128)(2,1)S(1)}, u32[]{:S(2)}, u32[]{:S(2)}) %collective-permute-start.30) | collective-permute-done | bytes 98336 | tf_op jit(solution)/shard_map/ppermute | solution.py:21
  (212 shorter events, 57.1 us)
Async XLA Ops:
  2.9 12.6 %collective-permute-start = (bf16[64,1024]{1,0:T(8,128)(2,1)S(1)}, bf16[64,1024]{1,0:T(8,128)(2,1)S(1)}, u32[]{:S(2)}, u32[]{:S(2)}) collective-permute-start(bf16[64,1024]{1,0:T(8,128)(2,1)S(1)} %fusion.51), channel_id=1, source_target_pairs={{0,2},{2,0},{4,6},{6,4},{8,10},{10,8},{12,14},{14,12},{16,18},{18,... | collective-permute-start | bytes 393224 | tf_op jit(solution)/shard_map/ppermute | solution.py:21
  3.4 13.5 %collective-permute-start.1 = (bf16[64,1024]{1,0:T(8,128)(2,1)S(1)}, bf16[64,1024]{1,0:T(8,128)(2,1)S(1)}, u32[]{:S(2)}, u32[]{:S(2)}) collective-permute-start(bf16[64,1024]{1,0:T(8,128)(2,1)S(1)} %fusion.51), channel_id=1, source_target_pairs={{0,4},{2,6},{4,0},{6,2},{8,12},{10,14},{12,8},{14,10},{16,20},{18,... | collective-permute-start | bytes 393224 | tf_op jit(solution)/shard_map/ppermute | solution.py:21
  5.9 11.1 %collective-permute-start.2 = (bf16[64,1024]{1,0:T(8,128)(2,1)S(1)}, bf16[64,1024]{1,0:T(8,128)(2,1)S(1)}, u32[]{:S(2)}, u32[]{:S(2)}) collective-permute-start(bf16[64,1024]{1,0:T(8,128)(2,1)S(1)} %fusion.51), channel_id=1, source_target_pairs={{0,6},{2,4},{4,2},{6,0},{8,14},{10,12},{12,10},{14,8},{16,22},{18,... | collective-permute-start | bytes 393224 | tf_op jit(solution)/shard_map/ppermute | solution.py:21
  8.1 9.0 %collective-permute-start.3 = (bf16[64,1024]{1,0:T(8,128)(2,1)S(1)}, bf16[64,1024]{1,0:T(8,128)(2,1)S(1)}, u32[]{:S(2)}, u32[]{:S(2)}) collective-permute-start(bf16[64,1024]{1,0:T(8,128)(2,1)S(1)} %fusion.53), channel_id=1, source_target_pairs={{0,8},{4,12},{8,0},{12,4},{16,24},{20,28},{24,16},{28,20},{1,9},{5... | collective-permute-start | bytes 393224 | tf_op jit(solution)/shard_map/ppermute | solution.py:21
  9.9 9.4 %collective-permute-start.4 = (bf16[64,1024]{1,0:T(8,128)(2,1)S(1)}, bf16[64,1024]{1,0:T(8,128)(2,1)}, u32[]{:S(2)}, u32[]{:S(2)}) collective-permute-start(bf16[64,1024]{1,0:T(8,128)(2,1)S(1)} %fusion.53), channel_id=1, source_target_pairs={{0,16},{4,20},{8,24},{12,28},{16,0},{20,4},{24,8},{28,12},{1,17},{... | collective-permute-start | bytes 393224 | tf_op jit(solution)/shard_map/ppermute | solution.py:21
  15.4 7.3 %collective-permute-start.5 = (bf16[64,1024]{1,0:T(8,128)(2,1)S(1)}, bf16[64,1024]{1,0:T(8,128)(2,1)}, u32[]{:S(2)}, u32[]{:S(2)}) collective-permute-start(bf16[64,1024]{1,0:T(8,128)(2,1)S(1)} %fusion.53), channel_id=1, source_target_pairs={{0,24},{4,28},{8,16},{12,20},{16,8},{20,12},{24,0},{28,4},{1,25},{... | collective-permute-start | bytes 393224 | tf_op jit(solution)/shard_map/ppermute | solution.py:21
  16.9 24.1 %collective-permute-start.13 = (bf16[512,512]{1,0:T(8,128)(2,1)S(1)}, bf16[512,512]{1,0:T(8,128)(2,1)S(1)}, u32[]{:S(2)}, u32[]{:S(2)}) collective-permute-start(bf16[512,512]{1,0:T(8,128)(2,1)S(1)} %bitcast.214), channel_id=1, source_target_pairs={{0,2},{2,0},{1,3},{3,1},{4,6},{6,4},{5,7},{7,5},{8,10},{10,8},{9,1... | collective-permute-start | bytes 1572872 | tf_op jit(solution)/shard_map/ppermute | solution.py:21
  24.3 6.9 %collective-permute-start.6 = (f32[2,64]{1,0:T(2,128)S(1)}, f32[2,64]{1,0:T(2,128)S(1)}, u32[]{:S(2)}, u32[]{:S(2)}) collective-permute-start(f32[2,64]{1,0:T(2,128)S(1)} %squeeze.155), channel_id=1, source_target_pairs={{0,4},{4,0},{8,12},{12,8},{16,20},{20,16},{24,28},{28,24},{1,5},{5... | collective-permute-start | bytes 1544 | tf_op jit(solution)/shard_map/ppermute | solution.py:21
  26.0 5.2 %collective-permute-start.7 = (f32[64]{0:T(128)S(1)}, f32[64]{0:T(128)S(1)}, u32[]{:S(2)}, u32[]{:S(2)}) collective-permute-start(f32[64]{0:T(128)S(1)} %get-tuple-element.32), channel_id=1, source_target_pairs={{0,8},{4,12},{8,0},{12,4},{16,24},{20,28},{24,16},{28,20},{1,9},{5... | collective-permute-start | bytes 776 | tf_op jit(solution)/shard_map/ppermute | solution.py:21
  28.7 4.4 %collective-permute-start.8 = (f32[64]{0:T(128)S(1)}, f32[64]{0:T(128)S(1)}, u32[]{:S(2)}, u32[]{:S(2)}) collective-permute-start(f32[64]{0:T(128)S(1)} %get-tuple-element.34), channel_id=1, source_target_pairs={{0,16},{4,20},{8,24},{12,28},{16,0},{20,4},{24,8},{28,12},{1,17},{... | collective-permute-start | bytes 776 | tf_op jit(solution)/shard_map/ppermute | solution.py:21
  29.7 5.3 %collective-permute-start.9 = (f32[64]{0:T(128)S(1)}, f32[64]{0:T(128)S(1)}, u32[]{:S(2)}, u32[]{:S(2)}) collective-permute-start(f32[64]{0:T(128)S(1)} %get-tuple-element.33), channel_id=1, source_target_pairs={{0,24},{4,28},{8,16},{12,20},{16,8},{20,12},{24,0},{28,4},{1,25},{... | collective-permute-start | bytes 776 | tf_op jit(solution)/shard_map/ppermute | solution.py:21
  31.2 9.8 %collective-permute-start.22 = (bf16[512,512]{1,0:T(8,128)(2,1)S(1)}, bf16[512,512]{1,0:T(8,128)(2,1)S(1)}, u32[]{:S(2)}, u32[]{:S(2)}) collective-permute-start(bf16[512,512]{1,0:T(8,128)(2,1)S(1)} %bitcast.215), channel_id=1, source_target_pairs={{0,2},{2,0},{1,3},{3,1},{4,6},{6,4},{5,7},{7,5},{8,10},{10,8},{9,1... | collective-permute-start | bytes 1572872 | tf_op jit(solution)/shard_map/ppermute | solution.py:21
  35.1 3.6 %collective-permute-start.10 = (f32[2,64]{1,0:T(2,128)S(1)}, f32[2,64]{1,0:T(2,128)S(1)}, u32[]{:S(2)}, u32[]{:S(2)}) collective-permute-start(f32[2,64]{1,0:T(2,128)S(1)} %multiply_select_fusion), channel_id=1, source_target_pairs={{0,1},{1,0},{2,3},{3,2},{4,5},{5,4},{6,7},{7,6},{8,9},{9,8},{10,11... | collective-permute-start | bytes 1544 | tf_op jit(solution)/shard_map/ppermute | solution.py:21
  37.0 3.0 %collective-permute-start.11 = (f32[2,64]{1,0:T(2,128)S(1)}, f32[2,64]{1,0:T(2,128)S(1)}, u32[]{:S(2)}, u32[]{:S(2)}) collective-permute-start(f32[2,64]{1,0:T(2,128)S(1)} %multiply_select_fusion), channel_id=1, source_target_pairs={{0,3},{1,2},{2,1},{3,0},{4,7},{5,6},{6,5},{7,4},{8,11},{9,10},{10,... | collective-permute-start | bytes 1544 | tf_op jit(solution)/shard_map/ppermute | solution.py:21
  37.0 3.0 %collective-permute-start.12 = (f32[2,64]{1,0:T(2,128)S(1)}, f32[2,64]{1,0:T(2,128)S(1)}, u32[]{:S(2)}, u32[]{:S(2)}) collective-permute-start(f32[2,64]{1,0:T(2,128)S(1)} %multiply_select_fusion), channel_id=1, source_target_pairs={{0,2},{2,0},{1,3},{3,1},{4,6},{6,4},{5,7},{7,5},{8,10},{10,8},{9,1... | collective-permute-start | bytes 1544 | tf_op jit(solution)/shard_map/ppermute | solution.py:21
  63.2 83.5 %collective-permute-start.35 = (bf16[2,2,2,64,768]{4,3,0,1,2:T(8,128)(2,1)}, bf16[2,2,2,64,768]{4,3,0,1,2:T(8,128)(2,1)}, u32[]{:S(2)}, u32[]{:S(2)}) collective-permute-start(bf16[2,2,2,64,768]{4,3,0,1,2:T(8,128)(2,1)} %bitcast.205), channel_id=1, source_target_pairs={{0,4},{4,0},{8,12},{12,8},{16,20},{20,16},{24,28},{28,24},{1,5},{5... | collective-permute-start | bytes 2359304 | tf_op jit(solution)/shard_map/ppermute | solution.py:21
  65.7 82.5 %collective-permute-start.39 = (bf16[2,2,2,64,768]{4,3,0,1,2:T(8,128)(2,1)}, bf16[2,2,2,64,768]{4,3,0,1,2:T(8,128)(2,1)}, u32[]{:S(2)}, u32[]{:S(2)}) collective-permute-start(bf16[2,2,2,64,768]{4,3,0,1,2:T(8,128)(2,1)} %bitcast.204), channel_id=1, source_target_pairs={{0,1},{1,0},{2,3},{3,2},{4,5},{5,4},{6,7},{7,6},{8,9},{9,8},{10,11... | collective-permute-start | bytes 2359304 | tf_op jit(solution)/shard_map/ppermute | solution.py:21
  68.0 16.5 %collective-permute-start.43 = (bf16[2,2,2,64,512]{4,3,0,2,1:T(8,128)(2,1)}, bf16[2,2,2,64,512]{4,3,0,2,1:T(8,128)(2,1)}, u32[]{:S(2)}, u32[]{:S(2)}) collective-permute-start(bf16[2,2,2,64,512]{4,3,0,2,1:T(8,128)(2,1)} %bitcast.209), channel_id=1, source_target_pairs={{0,8},{4,12},{8,0},{12,4},{16,24},{20,28},{24,16},{28,20},{1,9},{5... | collective-permute-start | bytes 1572872 | tf_op jit(solution)/shard_map/ppermute | solution.py:21
  70.2 85.6 %collective-permute-start.23 = (bf16[2,2,2,64,768]{4,3,0,1,2:T(8,128)(2,1)}, bf16[2,2,2,64,768]{4,3,0,1,2:T(8,128)(2,1)}, u32[]{:S(2)}, u32[]{:S(2)}) collective-permute-start(bf16[2,2,2,64,768]{4,3,0,1,2:T(8,128)(2,1)} %bitcast.207), channel_id=1, source_target_pairs={{0,4},{4,0},{8,12},{12,8},{16,20},{20,16},{24,28},{28,24},{1,5},{5... | collective-permute-start | bytes 2359304 | tf_op jit(solution)/shard_map/ppermute | solution.py:21
  76.9 4.5 %collective-permute-start.14 = (bf16[512,512]{1,0:T(8,128)(2,1)S(1)}, bf16[512,512]{1,0:T(8,128)(2,1)S(1)}, u32[]{:S(2)}, u32[]{:S(2)}) collective-permute-start(bf16[512,512]{1,0:T(8,128)(2,1)S(1)} %bitcast.223), channel_id=1, source_target_pairs={{0,2},{2,0},{1,3},{3,1},{4,6},{6,4},{5,7},{7,5},{8,10},{10,8},{9,1... | collective-permute-start | bytes 1572872 | tf_op jit(solution)/shard_map/ppermute | solution.py:21
  81.4 14.7 %collective-permute-start.31 = (bf16[2,2,2,64,512]{4,3,0,2,1:T(8,128)(2,1)}, bf16[2,2,2,64,512]{4,3,0,2,1:T(8,128)(2,1)S(1)}, u32[]{:S(2)}, u32[]{:S(2)}) collective-permute-start(bf16[2,2,2,64,512]{4,3,0,2,1:T(8,128)(2,1)} %bitcast.210), channel_id=1, source_target_pairs={{0,8},{4,12},{8,0},{12,4},{16,24},{20,28},{24,16},{28,20},{1,9},{5... | collective-permute-start | bytes 1572872 | tf_op jit(solution)/shard_map/ppermute | solution.py:21
  84.5 74.6 %collective-permute-start.27 = (bf16[2,2,2,64,768]{4,3,0,1,2:T(8,128)(2,1)}, bf16[2,2,2,64,768]{4,3,0,1,2:T(8,128)(2,1)}, u32[]{:S(2)}, u32[]{:S(2)}) collective-permute-start(bf16[2,2,2,64,768]{4,3,0,1,2:T(8,128)(2,1)} %bitcast.206), channel_id=1, source_target_pairs={{0,1},{1,0},{2,3},{3,2},{4,5},{5,4},{6,7},{7,6},{8,9},{9,8},{10,11... | collective-permute-start | bytes 2359304 | tf_op jit(solution)/shard_map/ppermute | solution.py:21
  96.1 5.4 %collective-permute-start.15 = (bf16[16,8,512]{2,1,0:T(8,128)(2,1)S(1)}, bf16[16,8,512]{2,1,0:T(8,128)(2,1)S(1)}, u32[]{:S(2)}, u32[]{:S(2)}) collective-permute-start(bf16[16,8,512]{2,1,0:T(8,128)(2,1)S(1)} %bitcast.236), channel_id=1, source_target_pairs={{0,4},{4,0},{8,12},{12,8},{16,20},{20,16},{24,28},{28,24},{1,5},{5... | collective-permute-start | bytes 393224 | tf_op jit(solution)/shard_map/ppermute | solution.py:21
  98.3 48.5 %copy-start.4 = (bf16[2,2,1,2,64,768]{5,4,3,2,1,0:T(8,128)(2,1)S(1)}, bf16[2,2,1,2,64,768]{5,4,3,2,1,0:T(8,128)(2,1)}, u32[]{:S(2)}) copy-start(bf16[2,2,1,2,64,768]{5,4,3,2,1,0:T(8,128)(2,1)} %get-tuple-element.6) | copy-start | bytes 2359300
  101.4 5.0 %collective-permute-start.16 = (bf16[16,8,512]{2,1,0:T(8,128)(2,1)S(1)}, bf16[16,8,512]{2,1,0:T(8,128)(2,1)S(1)}, u32[]{:S(2)}, u32[]{:S(2)}) collective-permute-start(bf16[16,8,512]{2,1,0:T(8,128)(2,1)S(1)} %bitcast.239), channel_id=1, source_target_pairs={{0,8},{4,12},{8,0},{12,4},{16,24},{20,28},{24,16},{28,20},{1,9},{5... | collective-permute-start | bytes 393224 | tf_op jit(solution)/shard_map/ppermute | solution.py:21
  106.4 5.9 %collective-permute-start.17 = (bf16[16,8,512]{2,1,0:T(8,128)(2,1)S(1)}, bf16[16,8,512]{2,1,0:T(8,128)(2,1)S(1)}, u32[]{:S(2)}, u32[]{:S(2)}) collective-permute-start(bf16[16,8,512]{2,1,0:T(8,128)(2,1)S(1)} %bitcast.238), channel_id=1, source_target_pairs={{0,12},{4,8},{8,4},{12,0},{16,28},{20,24},{24,20},{28,16},{1,13},{... | collective-permute-start | bytes 393224 | tf_op jit(solution)/shard_map/ppermute | solution.py:21
  112.3 5.9 %collective-permute-start.18 = (bf16[16,8,512]{2,1,0:T(8,128)(2,1)S(1)}, bf16[16,8,512]{2,1,0:T(8,128)(2,1)S(1)}, u32[]{:S(2)}, u32[]{:S(2)}) collective-permute-start(bf16[16,8,512]{2,1,0:T(8,128)(2,1)S(1)} %bitcast.237), channel_id=1, source_target_pairs={{0,16},{4,20},{8,24},{12,28},{16,0},{20,4},{24,8},{28,12},{1,17},{... | collective-permute-start | bytes 393224 | tf_op jit(solution)/shard_map/ppermute | solution.py:21
  118.1 7.4 %collective-permute-start.19 = (bf16[16,8,512]{2,1,0:T(8,128)(2,1)S(1)}, bf16[16,8,512]{2,1,0:T(8,128)(2,1)S(1)}, u32[]{:S(2)}, u32[]{:S(2)}) collective-permute-start(bf16[16,8,512]{2,1,0:T(8,128)(2,1)S(1)} %bitcast.235), channel_id=1, source_target_pairs={{0,20},{4,16},{8,28},{12,24},{16,4},{20,0},{24,12},{28,8},{1,21},{... | collective-permute-start | bytes 393224 | tf_op jit(solution)/shard_map/ppermute | solution.py:21
  125.5 9.5 %collective-permute-start.20 = (bf16[16,8,512]{2,1,0:T(8,128)(2,1)S(1)}, bf16[16,8,512]{2,1,0:T(8,128)(2,1)S(1)}, u32[]{:S(2)}, u32[]{:S(2)}) collective-permute-start(bf16[16,8,512]{2,1,0:T(8,128)(2,1)S(1)} %bitcast.234), channel_id=1, source_target_pairs={{0,24},{4,28},{8,16},{12,20},{16,8},{20,12},{24,0},{28,4},{1,25},{... | collective-permute-start | bytes 393224 | tf_op jit(solution)/shard_map/ppermute | solution.py:21
  135.1 7.9 %collective-permute-start.21 = (bf16[16,8,512]{2,1,0:T(8,128)(2,1)S(1)}, bf16[16,8,512]{2,1,0:T(8,128)(2,1)S(1)}, u32[]{:S(2)}, u32[]{:S(2)}) collective-permute-start(bf16[16,8,512]{2,1,0:T(8,128)(2,1)S(1)} %bitcast.233), channel_id=1, source_target_pairs={{0,28},{4,24},{8,20},{12,16},{16,12},{20,8},{24,4},{28,0},{1,29},{... | collective-permute-start | bytes 393224 | tf_op jit(solution)/shard_map/ppermute | solution.py:21
  142.9 10.5 %collective-permute-start.44 = (bf16[2,2,64,512]{3,2,0,1:T(8,128)(2,1)}, bf16[2,2,64,512]{3,2,0,1:T(8,128)(2,1)}, u32[]{:S(2)}, u32[]{:S(2)}) collective-permute-start(bf16[2,2,64,512]{3,2,0,1:T(8,128)(2,1)} %dynamic-slice_bitcast_fusion.4), channel_id=1, source_target_pairs={{0,4},{4,0},{8,12},{12,8},{16,20},{20,16},{24,28},{28,24},{1,5},{5... | collective-permute-start | bytes 786440 | tf_op jit(solution)/shard_map/ppermute | solution.py:21
  146.7 13.9 %collective-permute-start.32 = (bf16[2,2,64,512]{3,2,0,1:T(8,128)(2,1)}, bf16[2,2,64,512]{3,2,0,1:T(8,128)(2,1)S(1)}, u32[]{:S(2)}, u32[]{:S(2)}) collective-permute-start(bf16[2,2,64,512]{3,2,0,1:T(8,128)(2,1)} %dynamic-slice_bitcast_fusion.5), channel_id=1, source_target_pairs={{0,4},{4,0},{8,12},{12,8},{16,20},{20,16},{24,28},{28,24},{1,5},{5... | collective-permute-start | bytes 786440 | tf_op jit(solution)/shard_map/ppermute | solution.py:21
  148.2 35.9 %collective-permute-start.36 = (bf16[2,2,64,768]{3,2,0,1:T(8,128)(2,1)S(1)}, bf16[2,2,64,768]{3,2,0,1:T(8,128)(2,1)S(1)}, u32[]{:S(2)}, u32[]{:S(2)}) collective-permute-start(bf16[2,2,64,768]{3,2,0,1:T(8,128)(2,1)S(1)} %dynamic-slice_bitcast_fusion.1), channel_id=1, source_target_pairs={{0,1},{1,0},{2,3},{3,2},{4,5},{5,4},{6,7},{7,6},{8,9},{9,8},{10,11... | collective-permute-start | bytes 1179656 | tf_op jit(solution)/shard_map/ppermute | solution.py:21
  153.5 30.9 %collective-permute-start.40 = (bf16[2,2,64,768]{3,2,0,1:T(8,128)(2,1)S(1)}, bf16[2,2,64,768]{3,2,0,1:T(8,128)(2,1)S(1)}, u32[]{:S(2)}, u32[]{:S(2)}) collective-permute-start(bf16[2,2,64,768]{3,2,0,1:T(8,128)(2,1)S(1)} %dynamic-slice_bitcast_fusion), channel_id=1, source_target_pairs={{0,4},{4,0},{8,12},{12,8},{16,20},{20,16},{24,28},{28,24},{1,5},{5... | collective-permute-start | bytes 1179656 | tf_op jit(solution)/shard_map/ppermute | solution.py:21
  155.7 6.0 %collective-permute-start.45 = (bf16[2,64,512]{2,1,0:T(8,128)(2,1)S(1)}, bf16[2,64,512]{2,1,0:T(8,128)(2,1)S(1)}, u32[]{:S(2)}, u32[]{:S(2)}) collective-permute-start(bf16[2,64,512]{2,1,0:T(8,128)(2,1)S(1)} %dynamic-slice_bitcast_fusion.10), channel_id=1, source_target_pairs={{0,1},{1,0},{2,3},{3,2},{4,5},{5,4},{6,7},{7,6},{8,9},{9,8},{10,11... | collective-permute-start | bytes 393224 | tf_op jit(solution)/shard_map/ppermute | solution.py:21
  159.0 27.5 %collective-permute-start.24 = (bf16[2,2,64,768]{3,2,0,1:T(8,128)(2,1)S(1)}, bf16[2,2,64,768]{3,2,0,1:T(8,128)(2,1)S(1)}, u32[]{:S(2)}, u32[]{:S(2)}) collective-permute-start(bf16[2,2,64,768]{3,2,0,1:T(8,128)(2,1)S(1)} %dynamic-slice_bitcast_fusion.3), channel_id=1, source_target_pairs={{0,1},{1,0},{2,3},{3,2},{4,5},{5,4},{6,7},{7,6},{8,9},{9,8},{10,11... | collective-permute-start | bytes 1179656 | tf_op jit(solution)/shard_map/ppermute | solution.py:21
  160.7 26.1 %collective-permute-start.28 = (bf16[2,2,64,768]{3,2,0,1:T(8,128)(2,1)S(1)}, bf16[2,2,64,768]{3,2,0,1:T(8,128)(2,1)S(1)}, u32[]{:S(2)}, u32[]{:S(2)}) collective-permute-start(bf16[2,2,64,768]{3,2,0,1:T(8,128)(2,1)S(1)} %dynamic-slice_bitcast_fusion.2), channel_id=1, source_target_pairs={{0,4},{4,0},{8,12},{12,8},{16,20},{20,16},{24,28},{28,24},{1,5},{5... | collective-permute-start | bytes 1179656 | tf_op jit(solution)/shard_map/ppermute | solution.py:21
  161.7 6.5 %collective-permute-start.33 = (bf16[2,64,512]{2,1,0:T(8,128)(2,1)S(1)}, bf16[2,64,512]{2,1,0:T(8,128)(2,1)S(1)}, u32[]{:S(2)}, u32[]{:S(2)}) collective-permute-start(bf16[2,64,512]{2,1,0:T(8,128)(2,1)S(1)} %dynamic-slice_bitcast_fusion.11), channel_id=1, source_target_pairs={{0,1},{1,0},{2,3},{3,2},{4,5},{5,4},{6,7},{7,6},{8,9},{9,8},{10,11... | collective-permute-start | bytes 393224 | tf_op jit(solution)/shard_map/ppermute | solution.py:21
  168.3 6.2 %collective-permute-start.46 = (bf16[64,512]{1,0:T(8,128)(2,1)S(1)}, bf16[64,512]{1,0:T(8,128)(2,1)S(1)}, u32[]{:S(2)}, u32[]{:S(2)}) collective-permute-start(bf16[64,512]{1,0:T(8,128)(2,1)S(1)} %dynamic-slice_bitcast_fusion.16), channel_id=1, source_target_pairs={{0,16},{4,20},{8,24},{12,28},{16,0},{20,4},{24,8},{28,12},{1,17},{... | collective-permute-start | bytes 196616 | tf_op jit(solution)/shard_map/ppermute | solution.py:21
  174.5 9.6 %collective-permute-start.34 = (bf16[64,512]{1,0:T(8,128)(2,1)S(1)}, bf16[64,512]{1,0:T(8,128)(2,1)S(1)}, u32[]{:S(2)}, u32[]{:S(2)}) collective-permute-start(bf16[64,512]{1,0:T(8,128)(2,1)S(1)} %dynamic-slice_bitcast_fusion.17), channel_id=1, source_target_pairs={{0,16},{4,20},{8,24},{12,28},{16,0},{20,4},{24,8},{28,12},{1,17},{... | collective-permute-start | bytes 196616 | tf_op jit(solution)/shard_map/ppermute | solution.py:21
  184.3 5.7 %collective-permute-start.37 = (bf16[2,64,768]{2,1,0:T(8,128)(2,1)S(1)}, bf16[2,64,768]{2,1,0:T(8,128)(2,1)S(1)}, u32[]{:S(2)}, u32[]{:S(2)}) collective-permute-start(bf16[2,64,768]{2,1,0:T(8,128)(2,1)S(1)} %dynamic-slice_bitcast_fusion.7), channel_id=1, source_target_pairs={{0,8},{4,12},{8,0},{12,4},{16,24},{20,28},{24,16},{28,20},{1,9},{5... | collective-permute-start | bytes 589832 | tf_op jit(solution)/shard_map/ppermute | solution.py:21
  184.5 7.6 %collective-permute-start.41 = (bf16[2,64,768]{2,1,0:T(8,128)(2,1)S(1)}, bf16[2,64,768]{2,1,0:T(8,128)(2,1)S(1)}, u32[]{:S(2)}, u32[]{:S(2)}) collective-permute-start(bf16[2,64,768]{2,1,0:T(8,128)(2,1)S(1)} %dynamic-slice_bitcast_fusion.6), channel_id=1, source_target_pairs={{0,8},{4,12},{8,0},{12,4},{16,24},{20,28},{24,16},{28,20},{1,9},{5... | collective-permute-start | bytes 589832 | tf_op jit(solution)/shard_map/ppermute | solution.py:21
  186.7 7.5 %collective-permute-start.25 = (bf16[2,64,768]{2,1,0:T(8,128)(2,1)S(1)}, bf16[2,64,768]{2,1,0:T(8,128)(2,1)S(1)}, u32[]{:S(2)}, u32[]{:S(2)}) collective-permute-start(bf16[2,64,768]{2,1,0:T(8,128)(2,1)S(1)} %dynamic-slice_bitcast_fusion.9), channel_id=1, source_target_pairs={{0,8},{4,12},{8,0},{12,4},{16,24},{20,28},{24,16},{28,20},{1,9},{5... | collective-permute-start | bytes 589832 | tf_op jit(solution)/shard_map/ppermute | solution.py:21
  186.9 10.4 %collective-permute-start.29 = (bf16[2,64,768]{2,1,0:T(8,128)(2,1)S(1)}, bf16[2,64,768]{2,1,0:T(8,128)(2,1)S(1)}, u32[]{:S(2)}, u32[]{:S(2)}) collective-permute-start(bf16[2,64,768]{2,1,0:T(8,128)(2,1)S(1)} %dynamic-slice_bitcast_fusion.8), channel_id=1, source_target_pairs={{0,8},{4,12},{8,0},{12,4},{16,24},{20,28},{24,16},{28,20},{1,9},{5... | collective-permute-start | bytes 589832 | tf_op jit(solution)/shard_map/ppermute | solution.py:21
  190.1 7.5 %collective-permute-start.38 = (bf16[64,768]{1,0:T(8,128)(2,1)S(1)}, bf16[64,768]{1,0:T(8,128)(2,1)S(1)}, u32[]{:S(2)}, u32[]{:S(2)}) collective-permute-start(bf16[64,768]{1,0:T(8,128)(2,1)S(1)} %dynamic-slice_bitcast_fusion.13), channel_id=1, source_target_pairs={{0,16},{4,20},{8,24},{12,28},{16,0},{20,4},{24,8},{28,12},{1,17},{... | collective-permute-start | bytes 294920 | tf_op jit(solution)/shard_map/ppermute | solution.py:21
  192.2 7.7 %collective-permute-start.42 = (bf16[64,768]{1,0:T(8,128)(2,1)S(1)}, bf16[64,768]{1,0:T(8,128)(2,1)S(1)}, u32[]{:S(2)}, u32[]{:S(2)}) collective-permute-start(bf16[64,768]{1,0:T(8,128)(2,1)S(1)} %dynamic-slice_bitcast_fusion.12), channel_id=1, source_target_pairs={{0,16},{4,20},{8,24},{12,28},{16,0},{20,4},{24,8},{28,12},{1,17},{... | collective-permute-start | bytes 294920 | tf_op jit(solution)/shard_map/ppermute | solution.py:21
  194.3 6.7 %collective-permute-start.26 = (bf16[64,768]{1,0:T(8,128)(2,1)S(1)}, bf16[64,768]{1,0:T(8,128)(2,1)S(1)}, u32[]{:S(2)}, u32[]{:S(2)}) collective-permute-start(bf16[64,768]{1,0:T(8,128)(2,1)S(1)} %dynamic-slice_bitcast_fusion.15), channel_id=1, source_target_pairs={{0,16},{4,20},{8,24},{12,28},{16,0},{20,4},{24,8},{28,12},{1,17},{... | collective-permute-start | bytes 294920 | tf_op jit(solution)/shard_map/ppermute | solution.py:21
  197.5 5.6 %collective-permute-start.30 = (bf16[64,768]{1,0:T(8,128)(2,1)S(1)}, bf16[64,768]{1,0:T(8,128)(2,1)S(1)}, u32[]{:S(2)}, u32[]{:S(2)}) collective-permute-start(bf16[64,768]{1,0:T(8,128)(2,1)S(1)} %dynamic-slice_bitcast_fusion.14), channel_id=1, source_target_pairs={{0,16},{4,20},{8,24},{12,28},{16,0},{20,4},{24,8},{28,12},{1,17},{... | collective-permute-start | bytes 294920 | tf_op jit(solution)/shard_map/ppermute | solution.py:21
  (19 other events, 151.1 us)

commit v2 on v1

--- a/solution.py
+++ b/solution.py
@@ -1,6 +1,9 @@
+import itertools
 import jax
 import jax.numpy as jnp
 from jax import lax
+from jax.experimental import pallas as pl
+from jax.experimental.pallas import tpu as pltpu
 from jax.sharding import PartitionSpec as P
 
 
@@ -50,23 +53,174 @@
     return 0.5 * jnp.stack([of_shard[0] + of_text, of_shard[1]])
 
 
-def scatter_sum(block, order, axis_bits):
+def flip(index, mask):
+    out, bit = index, 1
+    while bit <= mask:
+        if mask & bit:
+            out = out + bit * (1 - 2 * ((index // bit) % 2))
+        bit *= 2
+    return out
+
+
+def grad_kernel(
+    axis_bits, orders, widths, subs, n_dp,
+    xt_ref, ct_ref, dh_ref, act_ref, boxed_ref,
+    up_ref, down_ref, landed_ref,
+    *scratch,
+):
+    bits, kinds = len(axis_bits), len(orders)
+    prods = scratch[:kinds]
+    recvs = [scratch[kinds + kind * bits : kinds + (kind + 1) * bits] for kind in range(kinds)]
+    send_sem, recv_sem, box_send, box_recv = scratch[kinds + kinds * bits :]
+    dp_at = lax.axis_index("dp")
+    group_at = lax.axis_index("group")
+    at = {"dp": dp_at, "group": group_at}
+
+    barrier = pltpu.get_barrier_semaphore()
+    partners = [{"dp": flip(dp_at, mask)} for mask in range(1, n_dp)]
+    partners.append({"group": 1 - group_at})
+    for partner in partners:
+        pl.semaphore_signal(
+            barrier, inc=1, device_id=partner, device_id_type=pl.DeviceIdType.MESH
+        )
+    pl.semaphore_wait(barrier, len(partners))
+
+    def pick(ref, lead, left, bit, value):
+        place = [slice(None)] * len(left)
+        place[left.index(bit)] = value
+        return ref.at[tuple(lead + place)]
+
+    def source(kind, step):
+        return prods[kind] if step == 0 else recvs[kind][step - 1]
+
+    def exchange(kind, turn, step):
+        bit = orders[kind][step]
+        left = [other for other in range(bits) if other not in orders[kind][:step]]
+        name, mask = axis_bits[bit]
+        mine = (at[name] // mask) % 2
+        ref = source(kind, step)
+        copy = pltpu.make_async_remote_copy(
+            src_ref=pick(ref, [turn], left, bit, 1 - mine),
+            dst_ref=recvs[kind][step].at[turn],
+            send_sem=send_sem.at[kind, turn, step],
+            recv_sem=recv_sem.at[kind, turn, step],
+            device_id={name: flip(at[name], mask)},
+            device_id_type=pl.DeviceIdType.MESH,
+        )
+        return copy, pick(ref, [turn], left, bit, mine)
+
+    turns = 2 * subs
+    starts = [subs * sum(widths[:kind]) for kind in range(kinds)]
+    flight = {}
+    for turn in range(turns):
+        rows_ref, cols_ref = ((xt_ref, dh_ref), (ct_ref, act_ref))[turn // subs]
+        for kind in range(kinds):
+            width = widths[kind]
+            low = starts[kind] + (turn % subs) * width
+            tile = rows_ref.shape[0] // 4
+
+            def multiply(tile_at, carry, kind=kind, turn=turn, low=low, width=width,
+                         rows_ref=rows_ref, cols_ref=cols_ref, tile=tile):
+                product = jnp.dot(
+                    rows_ref[pl.ds(pl.multiple_of(tile_at * tile, tile), tile), :],
+                    cols_ref[:, low : low + width],
+                    preferred_element_type=jnp.float32,
+                )
+                dest = prods[kind].at[turn, tile_at // 2, tile_at % 2]
+                dest[...] = product.astype(jnp.bfloat16).reshape(dest.shape)
+                return carry
+
+            lax.fori_loop(0, 4, multiply, 0)
+            copy, keep = exchange(kind, turn, 0)
+            copy.start()
+            flight[kind, turn] = (copy, keep)
+
+    boxes = []
+    for mask in range(1, n_dp):
+        box = pltpu.make_async_remote_copy(
+            src_ref=boxed_ref.at[mask],
+            dst_ref=landed_ref.at[mask],
+            send_sem=box_send.at[mask],
+            recv_sem=box_recv.at[mask],
+            device_id={"dp": flip(dp_at, mask)},
+            device_id_type=pl.DeviceIdType.MESH,
+        )
+        box.start()
+        boxes.append(box)
+    landed_ref[0] = boxed_ref[0]
+
+    sent = []
+    for step in range(bits):
+        for turn in range(turns):
+            for kind in range(kinds):
+                copy, keep = flight[kind, turn]
+                copy.wait_recv()
+                sent.append(copy)
+                came = recvs[kind][step].at[turn]
+                if step < bits - 1:
+                    for lead in itertools.product(*[range(size) for size in came.shape[:-2]]):
+                        came[lead] = (
+                            came[lead].astype(jnp.float32) + keep[lead].astype(jnp.float32)
+                        ).astype(jnp.bfloat16)
+                    copy, keep = exchange(kind, turn, step + 1)
+                    copy.start()
+                    flight[kind, turn] = (copy, keep)
+                else:
+                    out_ref = (up_ref, down_ref)[turn // subs]
+                    low = starts[kind] + (turn % subs) * widths[kind]
+                    out_ref[:, low : low + widths[kind]] = came[...].astype(jnp.float32) + keep[
+                        ...
+                    ].astype(jnp.float32)
+    for copy in sent:
+        copy.wait_send()
+    for box in boxes:
+        box.wait()
+
+
+def gradients(xt, ct, dh, act, boxed, axis_bits):
     bits = len(axis_bits)
-    width = block.shape[1]
-    cut = block.reshape((2,) * bits + (-1, width))
-    left = list(range(bits))
-    for step, bit in enumerate(order):
-        name, mask = axis_bits[bit]
-        mine = (lax.axis_index(name) // mask) % 2
-        at = left.index(bit)
-        left.remove(bit)
-        keep = lax.dynamic_index_in_dim(cut, mine, at, keepdims=False)
-        send = lax.dynamic_index_in_dim(cut, 1 - mine, at, keepdims=False)
-        came = swap(send, (name,), (mask,))
-        cut = keep.astype(jnp.float32) + came.astype(jnp.float32)
-        if step < bits - 1:
-            cut = cut.astype(jnp.bfloat16)
-    return cut
+    orders = part_orders(bits)
+    depth, hidden = dh.shape
+    subs = 2
+    widths = [hidden * 3 // 8 // subs, hidden * 3 // 8 // subs, hidden // 4 // subs]
+    turns = 2 * subs
+    rows = xt.shape[0] >> bits
+    n_dp = boxed.shape[0]
+    prods = [
+        pltpu.VMEM((turns,) + (2,) * bits + (rows, width), jnp.bfloat16) for width in widths
+    ]
+    recvs = [
+        pltpu.VMEM((turns,) + (2,) * (bits - 1 - step) + (rows, width), jnp.bfloat16)
+        for width in widths
+        for step in range(bits)
+    ]
+    vmem = pl.BlockSpec(memory_space=pltpu.VMEM)
+    kernel = lambda *refs: grad_kernel(axis_bits, orders, widths, subs, n_dp, *refs)
+    return pl.pallas_call(
+        kernel,
+        out_shape=(
+            jax.ShapeDtypeStruct((rows, hidden), jnp.float32),
+            jax.ShapeDtypeStruct((rows, hidden), jnp.float32),
+            jax.ShapeDtypeStruct(boxed.shape, boxed.dtype),
+        ),
+        in_specs=[vmem] * 5,
+        out_specs=(vmem, vmem, vmem),
+        scratch_shapes=prods
+        + recvs
+        + [
+            pltpu.SemaphoreType.DMA((len(orders), turns, bits)),
+            pltpu.SemaphoreType.DMA((len(orders), turns, bits)),
+            pltpu.SemaphoreType.DMA((n_dp,)),
+            pltpu.SemaphoreType.DMA((n_dp,)),
+        ],
+        compiler_params=pltpu.CompilerParams(
+            collective_id=0, has_side_effects=True, vmem_limit_bytes=44 * 1024 * 1024
+        ),
+        cost_estimate=pl.CostEstimate(
+            flops=4 * xt.shape[0] * depth * hidden, bytes_accessed=1 << 24, transcendentals=0
+        ),
+        name="grad_sums",
+    )(xt, ct, dh, act, boxed)
 
 
 def part_orders(bits):
@@ -149,13 +303,6 @@
         placer, out.reshape(slots, patch_rows * half_width), preferred_element_type=jnp.float32
     ).astype(jnp.bfloat16)
     boxed = boxed.reshape(n_dp, cap, patch_rows, half_width)
-    landed = jnp.stack(
-        [boxed[0]] + [swap(boxed[mask], ("dp",), (mask,)) for mask in range(1, n_dp)]
-    )
-    routed = landed[jnp.arange(n_dp, dtype=jnp.int32) ^ dp_at].reshape(
-        n_dp * cap, patch_rows, half_width
-    )
-
     share = jnp.where(tensor_at == 0, share, share[::-1])
     mine = share + swap(share, ("tensor",), (1,))
     partner = swap(share, ("group",), (1,)) + swap(share, ("tensor", "group"), (1, 1))
@@ -167,20 +314,15 @@
     row_weight = jnp.repeat(weight, patch_rows)[:, None]
 
     axis_bits = [("dp", 1 << bit) for bit in range(n_dp.bit_length() - 2, -1, -1)] + [("group", 1)]
-    hidden = w_up.shape[1]
-    edges = [0, hidden * 3 // 8, hidden * 3 // 4, hidden]
-    orders = part_orders(len(axis_bits))
-    sums = []
-    for rows, cols in ((x, grad_pre), (cot, act)):
-        scaled = (row_weight * cols.astype(jnp.float32)).astype(jnp.bfloat16)
-        parts = []
-        for order, low, high in zip(orders, edges[:-1], edges[1:]):
-            product = jnp.einsum(
-                "md,mf->df", rows, scaled[:, low:high], preferred_element_type=jnp.float32
-            ).astype(jnp.bfloat16)
-            parts.append(scatter_sum(product, order, axis_bits))
-        sums.append(jnp.concatenate(parts, axis=1))
-    return (learnability, routed, sums[0], sums[1])
+    dh = (row_weight * grad_pre).astype(jnp.bfloat16)
+    weighted_act = (row_weight * act.astype(jnp.float32)).astype(jnp.bfloat16)
+    grad_up, grad_down_t, landed = gradients(
+        x.T, cot.T, dh, weighted_act, boxed, axis_bits
+    )
+    routed = landed[jnp.arange(n_dp, dtype=jnp.int32) ^ dp_at].reshape(
+        n_dp * cap, patch_rows, half_width
+    )
+    return (learnability, routed, grad_up, grad_down_t)
 
 
 def solution(mesh):

time: 205 us -> 191 us (0.932)
  Pallas kernels: 0 us -> 104 us
  waiting for transfers between devices: 79.4 us -> 10.7 us
  starting transfers between devices: 58.7 us -> 16.2 us
  matrix products: 20 us -> 16.7 us
    pallas_call x0 -> x1, Pallas kernels: none -> 104 us  [gradients(): pl.pallas_call(kernel, out_shape=(jax.ShapeDtypeStruct((rows, hidden), jn...]
    ppermute x47 -> x16, waiting for transfers between devices: 79.4 us -> 10.7 us  [swap(): return lax.ppermute(block, names if len(names) > 1 else names[0], route)]
    ppermute x47 -> x16, starting transfers between devices: 58.7 us -> 16.2 us  [swap(): return lax.ppermute(block, names if len(names) > 1 else names[0], route)]
    dynamic_slice x12 -> x0, local copies, waits for them, and re-layouts: 10.4 us -> none  [the longest x6 5.5 us: scatter_sum(): send = lax.dynamic_index_in_dim(cut, 1 - mine, at, keepdims=False)]
    unnamed x56 -> x30, local copies, waits for them, and re-layouts: 3.49 us -> 11 us
    dot_general x6 -> x0, matrix products: 6.78 us -> none  [local(): jnp.einsum('md,mf->df', rows, scaled[:, low:high], preferred_element_type...]
    convert_element_type x19 -> x1, other arithmetic: 9.79 us -> 4.15 us  [local(): weighted_act = (row_weight * act.astype(jnp.float32)).astype(jnp.bfloat16)]
    transpose x0 -> x2, other arithmetic: none -> 2.22 us  [local(): grad_up, grad_down_t, landed = gradients(x.T, cot.T, dh, weighted_act, bo...]
  transfers between devices with their start and end apart: 47 -> 16, of which waited for: 24 -> 6; matrix products, arithmetic and copies ran while one was open for 19% -> 8% of each run, Pallas kernels for 0% -> 0%
where the time goes in v2:
time: 191 us; the launch traced here: 190 us
  Pallas kernels  104 us (54%)
  local copies, waits for them, and re-layouts  24.7 us (13%)
  other arithmetic  16.7 us (9%)
  matrix products  16.7 us (9%)
  starting transfers between devices  16.2 us (8%)
  waiting for transfers between devices  10.7 us (6%)
    pallas_call x1, Pallas kernels, gradients(): pl.pallas_call(kernel, out_shape=(jax.ShapeDtypeStruct((rows, hidden), jn...  104 us
    ppermute x16, starting transfers between devices, swap(): return lax.ppermute(block, names if len(names) > 1 else names[0], route)  16.2 us
    unnamed x30, local copies, waits for them, and re-layouts  11 us
    ppermute x16, waiting for transfers between devices, swap(): return lax.ppermute(block, names if len(names) > 1 else names[0], route)  10.7 us
    dot_general x1, matrix products, local(): jnp.einsum('md,fd->mf', cot, w_down, preferred_element_type=jnp.float32)  6.33 us
    convert_element_type x1, other arithmetic, local(): weighted_act = (row_weight * act.astype(jnp.float32)).astype(jnp.bfloat16)  4.15 us
  transfers between devices with their start and end apart: 16, of which 6 were waited for; matrix products, arithmetic and copies ran while one was open for 8% of the time, Pallas kernels for 0%

profile of v2, /device:TPU:0, one launch (start us, length us, event | category | flops | bytes accessed | tf_op | source)
XLA Modules:
  0.0 190.3 jit_solution(5688739103053113307)
XLA Ops:
  0.7 1.1 fusion.32
  1.8 1.0 fusion.33
  3.3 2.6 %collective-permute-start.1 = (bf16[64,1024]{1,0:T(8,128)(2,1)S(1)}, bf16[64,1024]{1,0:T(8,128)(2,1)}, u32[]{:S(2)}, u32[]{:S(2)}) collective-permute-start(bf16[64,1024]{1,0:T(8,128)(2,1)S(1)} %fusion.33), channel_id=1, source_target_pairs={{0,4},{2,6},{4,0},{6,2},{8,12},{10,14},{12,8},{14,10},{16,20},{18,... | collective-permute-start | bytes 393224 | tf_op jit(solution)/shard_map/ppermute | solution.py:24
  5.9 1.0 fusion.34
  7.0 1.0 fusion.35
  8.0 1.9 collective-permute-start.3
  9.9 2.6 %collective-permute-start.4 = (bf16[64,1024]{1,0:T(8,128)(2,1)S(1)}, bf16[64,1024]{1,0:T(8,128)(2,1)}, u32[]{:S(2)}, u32[]{:S(2)}) collective-permute-start(bf16[64,1024]{1,0:T(8,128)(2,1)S(1)} %fusion.35), channel_id=1, source_target_pairs={{0,16},{4,20},{8,24},{12,28},{16,0},{20,4},{24,8},{28,12},{1,17},{... | collective-permute-start | bytes 393224 | tf_op jit(solution)/shard_map/ppermute | solution.py:24
  13.1 0.7 compare_select_fusion.2
  13.8 0.9 convert_reduce_fusion
  14.7 0.7 multiply_add_fusion
  16.0 0.6 gather_fusion
  16.8 1.8 gather_fusion.1
  19.2 3.9 %collective-permute-done.5 = bf16[64,1024]{1,0:T(8,128)(2,1)} collective-permute-done((bf16[64,1024]{1,0:T(8,128)(2,1)S(1)}, bf16[64,1024]{1,0:T(8,128)(2,1)}, u32[]{:S(2)}, u32[]{:S(2)}) %collective-permute-start.5) | collective-permute-done | bytes 131104 | tf_op jit(solution)/shard_map/ppermute | solution.py:24
  23.1 1.7 fusion.53
  25.0 1.5 collective-permute-start.6
  26.6 2.2 %collective-permute-start.7 = (f32[64]{0:T(128)S(1)}, f32[64]{0:T(128)S(1)}, u32[]{:S(2)}, u32[]{:S(2)}) collective-permute-start(f32[64]{0:T(128)S(1)} %get-tuple-element.18), channel_id=1, source_target_pairs={{0,8},{4,12},{8,0},{12,4},{16,24},{20,28},{24,16},{28,20},{1,9},{5... | collective-permute-start | bytes 776 | tf_op jit(solution)/shard_map/ppermute | solution.py:24
  28.8 1.0 collective-permute-start.8
  29.9 1.4 collective-permute-start.9
  31.3 1.9 %collective-permute-done.8 = f32[64]{0:T(128)S(1)} collective-permute-done((f32[64]{0:T(128)S(1)}, f32[64]{0:T(128)S(1)}, u32[]{:S(2)}, u32[]{:S(2)}) %collective-permute-start.8) | collective-permute-done | bytes 288 | tf_op jit(solution)/shard_map/ppermute | solution.py:24
  33.3 1.9 %collective-permute-done.9 = f32[64]{0:T(128)S(1)} collective-permute-done((f32[64]{0:T(128)S(1)}, f32[64]{0:T(128)S(1)}, u32[]{:S(2)}, u32[]{:S(2)}) %collective-permute-start.9) | collective-permute-done | bytes 288 | tf_op jit(solution)/shard_map/ppermute | solution.py:24
  35.3 1.8 collective-permute-start.10
  37.5 1.4 collective-permute-done.10
  38.9 1.2 collective-permute-done.11
  40.2 0.8 select_reduce_fusion
  41.2 0.5 fusion.47
  41.8 1.5 broadcast_select_fusion.1
  43.2 1.0 fusion.12.refs_0_
  44.3 3.5 %multiply_convert_fusion.1 = (bf16[512,2048]{1,0:T(8,128)(2,1)S(1)}, f32[512,2048]{1,0:T(8,128)S(1)}) fusion(bf16[1024,2048]{1,0:T(8,128)(2,1)S(1)} %copy-done.11, bf16[512,512]{0,1:T(8,128)(2,1)S(1)} %get-tuple-element.25, bf16[512,512]{0,1:T(8,128)(2,1)S(1)} %get-tuple-element.26), kind=kOutput, calls=%fused_computation.13 | convolution fusion | flops 2159017984 | bytes 11534336 | tf_op jit(solution)/shard_map/dot_general | solution.py:279
  47.8 1.2 fusion.10.refs_1_
  48.9 6.3 %fusion.5 = f32[512,2048]{1,0:T(8,128)} fusion(f32[512,2048]{1,0:T(8,128)S(1)} %get-tuple-element.24, bf16[2048,1024]{1,0:T(8,128)(2,1)S(1)} %copy-done.12, bf16[512,512]{0,1:T(8,128)(2,1)S(1)} %get-tuple-element.13, bf16[512,512]{0,1:T(8,128)(2,1)S(1)} %get-tuple-element.12), kind=kOutput, calls=%fused_computation.11 | convolution fusion | flops 2169503744 | bytes 13631488 | tf_op jit(solution)/shard_map/md,fd->mf/dot_general | solution.py:283
  55.3 3.7 %fusion.56 = f32[512,1024]{1,0:T(8,128)} fusion(bf16[512,2048]{1,0:T(8,128)(2,1)S(1)} %get-tuple-element.23, bf16[2048,1024]{1,0:T(8,128)(2,1)S(1)} %copy-done.12), kind=kOutput, calls=%fused_computation.96 | convolution fusion | flops 2147483648 | bytes 8388608 | tf_op jit(solution)/shard_map/dot_general | solution.py:282
  59.0 3.0 %reshape.110 = f32[512,2,512]{2,1,0:T(2,128)S(1)} reshape(f32[512,1024]{1,0:T(8,128)} %fusion.56) | data formatting | bytes 4194304 | tf_op jit(solution)/shard_map/reshape | solution.py:286
  62.0 0.9 constant_dynamic-slice_fusion.1
  62.9 1.0 constant_dynamic-slice_fusion
  64.2 4.2 %multiply_convert_fusion = (bf16[512,2048]{1,0:T(8,128)(2,1)S(1)}, bf16[512,2048]{1,0:T(8,128)(2,1)}) fusion(bf16[512,2048]{1,0:T(8,128)(2,1)} %copy-done.10, f32[512]{0:T(512)S(1)} %mul.114, f32[512,2048]{1,0:T(8,128)S(1)} %copy-done.9), kind=kLoop, calls=%fused_computation.12 | loop fusion | flops 5242880 | bytes 10487808 | tf_op jit(solution)/shard_map/convert_element_type | solution.py:318
  68.4 1.1 fusion.8
  69.4 2.1 %reshape.111 = bf16[64,4096]{1,0:T(8,128)(2,1)} reshape(bf16[512,512]{1,0:T(8,128)(2,1)} %fusion.8) | data formatting | bytes 1048576 | tf_op jit(solution)/shard_map/reshape | solution.py:303
  71.5 1.5 convolution_convert_fusion
  73.4 1.6 copy-done.1
  75.0 1.2 copy-done.3
  76.2 1.2 copy-done.4
  77.4 103.7 %grad_sums.1 = (f32[64,2048]{1,0:T(8,128)S(1)}, f32[64,2048]{1,0:T(8,128)S(1)}, bf16[8,16,8,512]{3,2,1,0:T(8,128)(2,1)S(1)}) custom-call(bf16[1024,512]{1,0:T(8,128)(2,1)S(1)} %copy-done.3, bf16[1024,512]{1,0:T(8,128)(2,1)S(1)} %copy-done.4, bf16[512,2048]{1,0:T(8,128)(2,1)S(1)} %copy-done.1, bf16[512,2048]{1,0:T(8,128)(2,1)S(1)} %get-tuple-element.16.refs_3_, ...), custom_call_target="tpu_custom_call" | custom-call | flops 4294967296 | bytes 16777216 | tf_op jit(solution)/shard_map/grad_sums/pallas_call | solution.py:199
  181.2 1.0 copy-done.2
  182.1 0.8 copy-done.5
  183.0 0.8 copy-done.6
  183.8 2.8 %gather_fusion.2 = bf16[8,16,8,512]{3,2,1,0:T(8,128)(2,1)} fusion(bf16[8,16,8,512]{3,2,1,0:T(8,128)(2,1)} %copy-done.2, s32[1024]{0:T(1024)S(1)} %pad_clamp_fusion), kind=kCustom, calls=%fused_computation.2 | custom fusion | bytes 2097184 | tf_op jit(solution)/shard_map/gather | solution.py:322
  186.6 1.9 copy.43
  188.4 1.9 copy.44
  (65 shorter events, 3.7 us)
Async XLA Ops:
  0.6 15.3 %copy-start = (bf16[128,8,512]{2,1,0:T(8,128)(2,1)S(1)}, bf16[128,8,512]{2,1,0:T(8,128)(2,1)}, u32[]{:S(2)}) copy-start(bf16[128,8,512]{2,1,0:T(8,128)(2,1)} %param.15) | copy-start | bytes 3145732
  2.8 13.1 %collective-permute-start = (bf16[64,1024]{1,0:T(8,128)(2,1)S(1)}, bf16[64,1024]{1,0:T(8,128)(2,1)S(1)}, u32[]{:S(2)}, u32[]{:S(2)}) collective-permute-start(bf16[64,1024]{1,0:T(8,128)(2,1)S(1)} %fusion.33), channel_id=1, source_target_pairs={{0,2},{2,0},{4,6},{6,4},{8,10},{10,8},{12,14},{14,12},{16,18},{18,... | collective-permute-start | bytes 393224 | tf_op jit(solution)/shard_map/ppermute | solution.py:24
  3.3 15.6 %collective-permute-start.1 = (bf16[64,1024]{1,0:T(8,128)(2,1)S(1)}, bf16[64,1024]{1,0:T(8,128)(2,1)}, u32[]{:S(2)}, u32[]{:S(2)}) collective-permute-start(bf16[64,1024]{1,0:T(8,128)(2,1)S(1)} %fusion.33), channel_id=1, source_target_pairs={{0,4},{2,6},{4,0},{6,2},{8,12},{10,14},{12,8},{14,10},{16,20},{18,... | collective-permute-start | bytes 393224 | tf_op jit(solution)/shard_map/ppermute | solution.py:24
  5.9 13.1 %collective-permute-start.2 = (bf16[64,1024]{1,0:T(8,128)(2,1)S(1)}, bf16[64,1024]{1,0:T(8,128)(2,1)}, u32[]{:S(2)}, u32[]{:S(2)}) collective-permute-start(bf16[64,1024]{1,0:T(8,128)(2,1)S(1)} %fusion.33), channel_id=1, source_target_pairs={{0,6},{2,4},{4,2},{6,0},{8,14},{10,12},{12,10},{14,8},{16,22},{18,... | collective-permute-start | bytes 393224 | tf_op jit(solution)/shard_map/ppermute | solution.py:24
  8.0 11.0 %collective-permute-start.3 = (bf16[64,1024]{1,0:T(8,128)(2,1)S(1)}, bf16[64,1024]{1,0:T(8,128)(2,1)}, u32[]{:S(2)}, u32[]{:S(2)}) collective-permute-start(bf16[64,1024]{1,0:T(8,128)(2,1)S(1)} %fusion.35), channel_id=1, source_target_pairs={{0,8},{4,12},{8,0},{12,4},{16,24},{20,28},{24,16},{28,20},{1,9},{5... | collective-permute-start | bytes 393224 | tf_op jit(solution)/shard_map/ppermute | solution.py:24
  9.9 9.4 %collective-permute-start.4 = (bf16[64,1024]{1,0:T(8,128)(2,1)S(1)}, bf16[64,1024]{1,0:T(8,128)(2,1)}, u32[]{:S(2)}, u32[]{:S(2)}) collective-permute-start(bf16[64,1024]{1,0:T(8,128)(2,1)S(1)} %fusion.35), channel_id=1, source_target_pairs={{0,16},{4,20},{8,24},{12,28},{16,0},{20,4},{24,8},{28,12},{1,17},{... | collective-permute-start | bytes 393224 | tf_op jit(solution)/shard_map/ppermute | solution.py:24
  15.9 7.3 %collective-permute-start.5 = (bf16[64,1024]{1,0:T(8,128)(2,1)S(1)}, bf16[64,1024]{1,0:T(8,128)(2,1)}, u32[]{:S(2)}, u32[]{:S(2)}) collective-permute-start(bf16[64,1024]{1,0:T(8,128)(2,1)S(1)} %fusion.35), channel_id=1, source_target_pairs={{0,24},{4,28},{8,16},{12,20},{16,8},{20,12},{24,0},{28,4},{1,25},{... | collective-permute-start | bytes 393224 | tf_op jit(solution)/shard_map/ppermute | solution.py:24
  16.6 24.5 %copy-start.7 = (bf16[64,8,512]{2,1,0:T(8,128)(2,1)}, bf16[64,8,512]{2,1,0:T(8,128)(2,1)S(1)}, u32[]{:S(2)}) copy-start(bf16[64,8,512]{2,1,0:T(8,128)(2,1)S(1)} %gather_fusion) | copy-start | bytes 1572868
  18.9 22.9 %collective-permute-start.13 = (bf16[512,512]{0,1:T(8,128)(2,1)S(1)}, bf16[512,512]{0,1:T(8,128)(2,1)S(1)}, u32[]{:S(2)}, u32[]{:S(2)}) collective-permute-start(bf16[512,512]{0,1:T(8,128)(2,1)S(1)} %copy.26), channel_id=1, source_target_pairs={{0,2},{2,0},{1,3},{3,1},{4,6},{6,4},{5,7},{7,5},{8,10},{10,8},{9,1... | collective-permute-start | bytes 1572872 | tf_op jit(solution)/shard_map/ppermute | solution.py:24
  25.0 6.4 %collective-permute-start.6 = (f32[2,64]{1,0:T(2,128)S(1)}, f32[2,64]{1,0:T(2,128)S(1)}, u32[]{:S(2)}, u32[]{:S(2)}) collective-permute-start(f32[2,64]{1,0:T(2,128)S(1)} %squeeze.29), channel_id=1, source_target_pairs={{0,4},{4,0},{8,12},{12,8},{16,20},{20,16},{24,28},{28,24},{1,5},{5... | collective-permute-start | bytes 1544 | tf_op jit(solution)/shard_map/ppermute | solution.py:24
  26.6 4.7 %collective-permute-start.7 = (f32[64]{0:T(128)S(1)}, f32[64]{0:T(128)S(1)}, u32[]{:S(2)}, u32[]{:S(2)}) collective-permute-start(f32[64]{0:T(128)S(1)} %get-tuple-element.18), channel_id=1, source_target_pairs={{0,8},{4,12},{8,0},{12,4},{16,24},{20,28},{24,16},{28,20},{1,9},{5... | collective-permute-start | bytes 776 | tf_op jit(solution)/shard_map/ppermute | solution.py:24
  28.8 4.4 %collective-permute-start.8 = (f32[64]{0:T(128)S(1)}, f32[64]{0:T(128)S(1)}, u32[]{:S(2)}, u32[]{:S(2)}) collective-permute-start(f32[64]{0:T(128)S(1)} %get-tuple-element.20), channel_id=1, source_target_pairs={{0,16},{4,20},{8,24},{12,28},{16,0},{20,4},{24,8},{28,12},{1,17},{... | collective-permute-start | bytes 776 | tf_op jit(solution)/shard_map/ppermute | solution.py:24
  29.9 5.3 %collective-permute-start.9 = (f32[64]{0:T(128)S(1)}, f32[64]{0:T(128)S(1)}, u32[]{:S(2)}, u32[]{:S(2)}) collective-permute-start(f32[64]{0:T(128)S(1)} %get-tuple-element.19), channel_id=1, source_target_pairs={{0,24},{4,28},{8,16},{12,20},{16,8},{20,12},{24,0},{28,4},{1,25},{... | collective-permute-start | bytes 776 | tf_op jit(solution)/shard_map/ppermute | solution.py:24
  31.3 10.5 %collective-permute-start.14 = (bf16[512,512]{0,1:T(8,128)(2,1)S(1)}, bf16[512,512]{0,1:T(8,128)(2,1)}, u32[]{:S(2)}, u32[]{:S(2)}) collective-permute-start(bf16[512,512]{0,1:T(8,128)(2,1)S(1)} %copy.29), channel_id=1, source_target_pairs={{0,2},{2,0},{1,3},{3,1},{4,6},{6,4},{5,7},{7,5},{8,10},{10,8},{9,1... | collective-permute-start | bytes 1572872 | tf_op jit(solution)/shard_map/ppermute | solution.py:24
  35.3 3.6 %collective-permute-start.10 = (f32[2,64]{1,0:T(2,128)S(1)}, f32[2,64]{1,0:T(2,128)S(1)}, u32[]{:S(2)}, u32[]{:S(2)}) collective-permute-start(f32[2,64]{1,0:T(2,128)S(1)} %multiply_select_fusion), channel_id=1, source_target_pairs={{0,1},{1,0},{2,3},{3,2},{4,5},{5,4},{6,7},{7,6},{8,9},{9,8},{10,11... | collective-permute-start | bytes 1544 | tf_op jit(solution)/shard_map/ppermute | solution.py:24
  37.1 3.0 %collective-permute-start.11 = (f32[2,64]{1,0:T(2,128)S(1)}, f32[2,64]{1,0:T(2,128)S(1)}, u32[]{:S(2)}, u32[]{:S(2)}) collective-permute-start(f32[2,64]{1,0:T(2,128)S(1)} %multiply_select_fusion), channel_id=1, source_target_pairs={{0,3},{1,2},{2,1},{3,0},{4,7},{5,6},{6,5},{7,4},{8,11},{9,10},{10,... | collective-permute-start | bytes 1544 | tf_op jit(solution)/shard_map/ppermute | solution.py:24
  37.1 3.0 %collective-permute-start.12 = (f32[2,64]{1,0:T(2,128)S(1)}, f32[2,64]{1,0:T(2,128)S(1)}, u32[]{:S(2)}, u32[]{:S(2)}) collective-permute-start(f32[2,64]{1,0:T(2,128)S(1)} %multiply_select_fusion), channel_id=1, source_target_pairs={{0,2},{2,0},{1,3},{3,1},{4,6},{6,4},{5,7},{7,5},{8,10},{10,8},{9,1... | collective-permute-start | bytes 1544 | tf_op jit(solution)/shard_map/ppermute | solution.py:24
  41.2 3.0 %copy-start.11 = (bf16[1024,2048]{1,0:T(8,128)(2,1)S(1)}, bf16[1024,2048]{1,0:T(8,128)(2,1)}, u32[]{:S(2)}) copy-start(bf16[1024,2048]{1,0:T(8,128)(2,1)} %param.17) | copy-start | bytes 12582916
  44.3 4.7 %copy-start.12 = (bf16[2048,1024]{1,0:T(8,128)(2,1)S(1)}, bf16[2048,1024]{1,0:T(8,128)(2,1)}, u32[]{:S(2)}) copy-start(bf16[2048,1024]{1,0:T(8,128)(2,1)} %param.18) | copy-start | bytes 12582916
  47.7 7.5 %copy-start.10 = (bf16[512,2048]{1,0:T(8,128)(2,1)}, bf16[512,2048]{1,0:T(8,128)(2,1)S(1)}, u32[]{:S(2)}) copy-start(bf16[512,2048]{1,0:T(8,128)(2,1)S(1)} %get-tuple-element.23) | copy-start | bytes 6291460
  62.0 2.2 %copy-start.9 = (f32[512,2048]{1,0:T(8,128)S(1)}, f32[512,2048]{1,0:T(8,128)}, u32[]{:S(2)}) copy-start(f32[512,2048]{1,0:T(8,128)} %fusion.5) | copy-start | bytes 12582916
  64.0 4.3 %copy-start.8 = (bf16[64,8,512]{2,1,0:T(8,128)(2,1)S(1)}, bf16[64,8,512]{2,1,0:T(8,128)(2,1)}, u32[]{:S(2)}) copy-start(bf16[64,8,512]{2,1,0:T(8,128)(2,1)} %copy-done.7) | copy-start | bytes 1572868
  64.0 4.3 %collective-permute-start.15 = (bf16[512,512]{1,0:T(8,128)(2,1)S(1)}, bf16[512,512]{1,0:T(8,128)(2,1)S(1)}, u32[]{:S(2)}, u32[]{:S(2)}) collective-permute-start(bf16[512,512]{1,0:T(8,128)(2,1)S(1)} %bitcast.45), channel_id=1, source_target_pairs={{0,2},{2,0},{1,3},{3,1},{4,6},{6,4},{5,7},{7,5},{8,10},{10,8},{9,1... | collective-permute-start | bytes 1572872 | tf_op jit(solution)/shard_map/ppermute | solution.py:24
  73.4 1.6 copy-start.1
  75.0 1.2 copy-start.3
  76.2 1.2 copy-start.4
  181.2 1.0 copy-start.2
  182.1 0.8 copy-start.5
  183.0 0.8 copy-start.6

commit v3 on v2

--- a/solution.py
+++ b/solution.py
@@ -24,35 +24,6 @@
     return lax.ppermute(block, names if len(names) > 1 else names[0], route)
 
 
-def unit_rows(block):
-    wide = block.astype(jnp.float32)
-    return (wide * lax.rsqrt(jnp.sum(wide * wide, axis=1, keepdims=True) + 1e-06)).astype(
-        jnp.bfloat16
-    )
-
-
-def loss_parts(image, text, temp, bias):
-    rows = image.shape[0]
-    far = lax.axis_size("dp") // 2
-    near_masks = [(0, 0), (0, 1), (1, 0), (1, 1)]
-    images = [image] + [swap(image, ("dp", "tensor"), mask) for mask in near_masks[1:]]
-    texts = [text] + [swap(text, ("dp",), (2 * mask,)) for mask in range(1, far)]
-    img = jnp.concatenate(images, axis=0)
-    txt = jnp.concatenate(texts, axis=0)
-    scores = temp * jnp.einsum("rd,kd->rk", img, txt, preferred_element_type=jnp.float32) + bias
-    at_row = jnp.arange(img.shape[0], dtype=jnp.int32)[:, None]
-    at_col = jnp.arange(txt.shape[0], dtype=jnp.int32)[None, :]
-    same = (at_row == at_col) & (at_row < rows)
-    terms = jax.nn.softplus(jnp.where(same, -scores, scores))
-    by_image = jnp.sum(terms, axis=1).reshape(2, 2, rows)
-    by_text = jnp.sum(terms, axis=0).reshape(far, rows)
-    of_shard = by_image[0] + swap(by_image[1], ("dp",), (1,))
-    of_text = by_text[0]
-    for mask in range(1, far):
-        of_text = of_text + swap(by_text[mask], ("dp",), (2 * mask,))
-    return 0.5 * jnp.stack([of_shard[0] + of_text, of_shard[1]])
-
-
 def flip(index, mask):
     out, bit = index, 1
     while bit <= mask:
@@ -60,6 +31,150 @@
             out = out + bit * (1 - 2 * ((index // bit) % 2))
         bit *= 2
     return out
+
+
+def loss_kernel(
+    n_dp, temp, bias,
+    ref_img, ref_txt, own_img, own_txt, half_x, half_cot,
+    score_ref, other_x, other_cot,
+    imgs, txts, row_out, row_in, text_out, text_in, share, share_in, send_sem, recv_sem,
+):
+    rows, width = own_img.shape
+    far = n_dp // 2
+    dp_at, tensor_at = lax.axis_index("dp"), lax.axis_index("tensor")
+    group_at = lax.axis_index("group")
+    over_tensor = {"tensor": 1 - tensor_at}
+    near = [
+        over_tensor,
+        {"dp": flip(dp_at, 1)},
+        {"dp": flip(dp_at, 1), "tensor": 1 - tensor_at},
+    ]
+    across = [{"dp": flip(dp_at, 2 * mask)} for mask in range(1, far)]
+    models = [{"group": 1 - group_at}, {"group": 1 - group_at, "tensor": 1 - tensor_at}]
+    partners = near + across + models
+    barrier = pltpu.get_barrier_semaphore()
+    for partner in partners:
+        pl.semaphore_signal(
+            barrier, inc=1, device_id=partner, device_id_type=pl.DeviceIdType.MESH
+        )
+
+    def put(value, dest):
+        wide = value[...].astype(jnp.float32)
+        total = jnp.sum(wide * wide, axis=1, keepdims=True)
+        dest[:, : value.shape[1]] = (wide * lax.rsqrt(total + 1e-06)).astype(jnp.bfloat16)
+
+    @pl.when(group_at == 0)
+    def _():
+        for raw, dest in ((ref_img, imgs.at[0]), (ref_txt, txts.at[0])):
+            dest[...] = jnp.zeros((rows, width), jnp.bfloat16)
+            put(raw, dest)
+
+    @pl.when(group_at == 1)
+    def _():
+        put(own_img, imgs.at[0])
+        put(own_txt, txts.at[0])
+
+    pl.semaphore_wait(barrier, len(partners))
+    used = [0]
+
+    def send(src, dest, partner):
+        at = used[0]
+        used[0] += 1
+        copy = pltpu.make_async_remote_copy(
+            src_ref=src,
+            dst_ref=dest,
+            send_sem=send_sem.at[at],
+            recv_sem=recv_sem.at[at],
+            device_id=partner,
+            device_id_type=pl.DeviceIdType.MESH,
+        )
+        copy.start()
+        return copy
+
+    copies = [send(txts.at[0], txts.at[m], to) for m, to in enumerate(across, 1)]
+    copies += [send(imgs.at[0], imgs.at[m], to) for m, to in enumerate(near, 1)]
+    wide_copies = [send(half_x, other_x, over_tensor), send(half_cot, other_cot, over_tensor)]
+    for copy in copies:
+        copy.wait()
+
+    def sums(long, short, has_own):
+        scores = temp * lax.dot_general(
+            long, short, (((1,), (1,)), ((), ())), preferred_element_type=jnp.float32
+        ) + bias
+        if has_own:
+            at_row = lax.broadcasted_iota(jnp.int32, scores.shape, 0)
+            at_col = lax.broadcasted_iota(jnp.int32, scores.shape, 1)
+            scores = jnp.where(at_row == at_col, -scores, scores)
+        terms = jnp.maximum(scores, 0.0) + jnp.log1p(jnp.exp(-jnp.abs(scores)))
+        total = jnp.sum(terms, axis=0, keepdims=True)
+        total = jnp.concatenate([total, jnp.zeros((1, 128 - rows), jnp.float32)], axis=1)
+        return jnp.broadcast_to(total, (8, 128))
+
+    all_txt = txts[...].reshape(far * rows, width)
+    all_img = imgs[...].reshape(4 * rows, width)
+    by_image = [sums(all_txt, imgs[m], m == 0) for m in range(4)]
+    row_out[0] = by_image[2]
+    row_out[1] = by_image[3]
+    copies = [send(row_out, row_in, near[1])]
+    for m in range(1, far):
+        text_out[m] = sums(all_img, txts[m], False)
+        copies.append(send(text_out.at[m], text_in.at[m], across[m - 1]))
+    own_text = sums(all_img, txts[0], True)
+    for copy in copies:
+        copy.wait()
+    for m in range(1, far):
+        own_text = own_text + text_in[m]
+    share[0] = 0.5 * (by_image[0] + row_in[0] + own_text)
+    share[1] = 0.5 * (by_image[1] + row_in[1])
+    copies = [
+        send(share, share_in.at[m], to) for m, to in enumerate([over_tensor] + models)
+    ]
+    for copy in copies:
+        copy.wait()
+    for half in range(2):
+        mine = share[half] + share_in[0, 1 - half]
+        partner = share_in[1, half] + share_in[2, 1 - half]
+        score_ref[half] = jnp.where(group_at == 0, partner - mine, mine - partner)
+    for copy in wide_copies:
+        copy.wait()
+
+
+def shard_learnability(ref_img, ref_txt, own_img, own_txt, half_x, half_cot, n_dp):
+    rows, width = own_img.shape
+    far = n_dp // 2
+    copies = 3 + (far - 1) + 2 + 1 + (far - 1) + 3
+    vmem = pl.BlockSpec(memory_space=pltpu.VMEM)
+    kernel = lambda *refs: loss_kernel(n_dp, 10.0, -5.0, *refs)
+    tile = (8, 128)
+    return pl.pallas_call(
+        kernel,
+        out_shape=(
+            jax.ShapeDtypeStruct((2,) + tile, jnp.float32),
+            jax.ShapeDtypeStruct(half_x.shape, half_x.dtype),
+            jax.ShapeDtypeStruct(half_cot.shape, half_cot.dtype),
+        ),
+        in_specs=[vmem] * 6,
+        out_specs=(vmem, vmem, vmem),
+        scratch_shapes=[
+            pltpu.VMEM((4, rows, width), jnp.bfloat16),
+            pltpu.VMEM((far, rows, width), jnp.bfloat16),
+            pltpu.VMEM((2,) + tile, jnp.float32),
+            pltpu.VMEM((2,) + tile, jnp.float32),
+            pltpu.VMEM((far,) + tile, jnp.float32),
+            pltpu.VMEM((far,) + tile, jnp.float32),
+            pltpu.VMEM((2,) + tile, jnp.float32),
+            pltpu.VMEM((3, 2) + tile, jnp.float32),
+            pltpu.SemaphoreType.DMA((copies,)),
+            pltpu.SemaphoreType.DMA((copies,)),
+        ],
+        compiler_params=pltpu.CompilerParams(
+            collective_id=1, has_side_effects=True, vmem_limit_bytes=24 * 1024 * 1024
+        ),
+        cost_estimate=pl.CostEstimate(
+            flops=16 * rows * rows * far * width, bytes_accessed=1 << 22, transcendentals=1 << 18
+        ),
+        name="pair_losses",
+    )(ref_img, ref_txt, own_img, own_txt, half_x, half_cot)
 
 
 def grad_kernel(
@@ -139,7 +254,7 @@
     for mask in range(1, n_dp):
         box = pltpu.make_async_remote_copy(
             src_ref=boxed_ref.at[mask],
-            dst_ref=landed_ref.at[mask],
+            dst_ref=landed_ref.at[dp_at],
             send_sem=box_send.at[mask],
             recv_sem=box_recv.at[mask],
             device_id={"dp": flip(dp_at, mask)},
@@ -147,7 +262,7 @@
         )
         box.start()
         boxes.append(box)
-    landed_ref[0] = boxed_ref[0]
+    landed_ref[dp_at] = boxed_ref[0]
 
     sent = []
     for step in range(bits):
@@ -229,7 +344,7 @@
     return [
         [near, group, next_near] + rest,
         [group, near, next_near] + rest,
-        [next_near, near, group] + rest,
+        [next_near, group, near] + rest,
     ]
 
 
@@ -246,21 +361,9 @@
     sel_index,
     sel_dest,
 ):
-    group_at = lax.axis_index("group")
     tensor_at = lax.axis_index("tensor")
     dp_at = lax.axis_index("dp")
     n_dp = lax.axis_size("dp")
-    extra = learner_image.shape[1] - ref_image.shape[1]
-    is_ref = group_at == 0
-
-    def own_model(ref_block, learner_block):
-        ref_block = jnp.pad(ref_block, ((0, 0), (0, extra)))
-        return unit_rows(jnp.where(is_ref, ref_block, learner_block))
-
-    share = loss_parts(
-        own_model(ref_image, learner_image), own_model(ref_text, learner_text), 10.0, -5.0
-    )
-
     slots = sel_index.shape[0]
     cap = max(2, 2 * slots // n_dp)
     patch_rows, half_width = (patches.shape[1], patches.shape[2])
@@ -268,26 +371,30 @@
     half_x = patches[sel_index].reshape(count, half_width)
     half_cot = cotangent[sel_index].reshape(count, half_width)
 
-    def widen(half):
-        other = swap(half, ("tensor",), (1,))
+    scores, other_x, other_cot = shard_learnability(
+        ref_image, ref_text, learner_image, learner_text, half_x, half_cot, n_dp
+    )
+
+    def widen(half, other):
         return jnp.concatenate(
             [jnp.where(tensor_at == 0, half, other), jnp.where(tensor_at == 0, other, half)], axis=1
         )
 
-    x = widen(half_x)
-    cot = widen(half_cot)
+    x = widen(half_x, other_x)
+    cot = widen(half_cot, other_cot)
     pre = jnp.dot(x, w_up, preferred_element_type=jnp.float32)
     act_full, gelu_back = jax.vjp(jax.nn.gelu, pre)
     act = lax.optimization_barrier(act_full.astype(jnp.bfloat16))
-    partial_out = jnp.dot(act, w_down, preferred_element_type=jnp.float32)
+    def down(side):
+        columns = lax.dynamic_slice_in_dim(w_down, side * half_width, half_width, 1)
+        return jnp.dot(act, columns, preferred_element_type=jnp.float32)
+
+    came = swap(down(1 - tensor_at).astype(jnp.bfloat16), ("tensor",), (1,))
+    out = (half_x.astype(jnp.float32) + (down(tensor_at) + came.astype(jnp.float32))).astype(
+        jnp.bfloat16
+    )
     back = jnp.einsum("md,fd->mf", cot, w_down, preferred_element_type=jnp.float32)
     grad_pre = lax.optimization_barrier(gelu_back(back)[0])
-
-    halves = partial_out.reshape(count, 2, half_width)
-    keep = lax.dynamic_index_in_dim(halves, tensor_at, 1, keepdims=False)
-    send = lax.dynamic_index_in_dim(halves, 1 - tensor_at, 1, keepdims=False)
-    came = swap(send.astype(jnp.bfloat16), ("tensor",), (1,))
-    out = (half_x.astype(jnp.float32) + (keep + came.astype(jnp.float32))).astype(jnp.bfloat16)
 
     live = jnp.arange(slots, dtype=jnp.int32) < counts[0]
     target = sel_dest[:, 0]
@@ -296,20 +403,26 @@
         (earlier & (target[:, None] == target[None, :]) & live[None, :]).astype(jnp.int32), axis=1
     )
     bucket = (target ^ dp_at) * cap + rank
+    slot_row = jnp.repeat(jnp.where(live, bucket, -1), patch_rows) * patch_rows + jnp.tile(
+        jnp.arange(patch_rows, dtype=jnp.int32), slots
+    )
     placer = (
-        (jnp.arange(n_dp * cap, dtype=jnp.int32)[:, None] == bucket[None, :]) & live[None, :]
+        jnp.arange(n_dp * cap * patch_rows, dtype=jnp.int32)[:, None] == slot_row[None, :]
     ).astype(jnp.bfloat16)
-    boxed = jnp.dot(
-        placer, out.reshape(slots, patch_rows * half_width), preferred_element_type=jnp.float32
-    ).astype(jnp.bfloat16)
-    boxed = boxed.reshape(n_dp, cap, patch_rows, half_width)
-    share = jnp.where(tensor_at == 0, share, share[::-1])
-    mine = share + swap(share, ("tensor",), (1,))
-    partner = swap(share, ("group",), (1,)) + swap(share, ("tensor", "group"), (1, 1))
-    shard_scores = jnp.where(is_ref, partner - mine, mine - partner)
-    learnability = lax.dynamic_index_in_dim(shard_scores, tensor_at, 0, keepdims=False)
+    boxed = jnp.dot(placer, out, preferred_element_type=jnp.float32).astype(jnp.bfloat16)
+    boxed = boxed.reshape(n_dp, cap * patch_rows, half_width)
+
+    pairs = learner_image.shape[0]
+    learnability = scores[0, 0, :pairs]
+    other_scores = scores[1, 0, :pairs]
+    shard_scores = jnp.concatenate(
+        [
+            jnp.where(tensor_at == 0, learnability, other_scores),
+            jnp.where(tensor_at == 0, other_scores, learnability),
+        ]
+    )
     picked = sel_index[:, None] == jnp.arange(patches.shape[0], dtype=jnp.int32)[None, :]
-    score_sel = jnp.sum(jnp.where(picked, shard_scores.reshape(1, -1), 0.0), axis=1)
+    score_sel = jnp.sum(jnp.where(picked, shard_scores[None, :], 0.0), axis=1)
     weight = jnp.where(live, jax.nn.sigmoid(score_sel), 0.0)
     row_weight = jnp.repeat(weight, patch_rows)[:, None]
 
@@ -319,9 +432,7 @@
     grad_up, grad_down_t, landed = gradients(
         x.T, cot.T, dh, weighted_act, boxed, axis_bits
     )
-    routed = landed[jnp.arange(n_dp, dtype=jnp.int32) ^ dp_at].reshape(
-        n_dp * cap, patch_rows, half_width
-    )
+    routed = landed.reshape(n_dp * cap, patch_rows, half_width)
     return (learnability, routed, grad_up, grad_down_t)
 
 

time: 191 us -> 175 us (0.916)
  starting transfers between devices: 16.2 us -> 0.1 us
  Pallas kernels: 104 us -> 119 us
  waiting for transfers between devices: 10.7 us -> 0.01 us
  local copies, waits for them, and re-layouts: 24.7 us -> 14.8 us
  matrix products: 16.7 us -> 25.9 us
  other arithmetic: 16.7 us -> 13.3 us
    pallas_call x0 -> x1, Pallas kernels: none -> 25.6 us  [shard_learnability(): pl.pallas_call(kernel, out_shape=(jax.ShapeDtypeStruct((2,) + tile, jnp.f...]
    ppermute x16 -> x1, starting transfers between devices: 16.2 us -> 0.1 us  [swap(): return lax.ppermute(block, names if len(names) > 1 else names[0], route)]
    ppermute x16 -> x1, waiting for transfers between devices: 10.7 us -> 0.01 us  [swap(): return lax.ppermute(block, names if len(names) > 1 else names[0], route)]
    pallas_call x1, Pallas kernels: 104 us -> 93.7 us  [gradients(): pl.pallas_call(kernel, out_shape=(jax.ShapeDtypeStruct((rows, hidden), jn...]
    reshape x2 -> x0, local copies, waits for them, and re-layouts: 5.1 us -> none  [the longest x1 3.03 us: local(): halves = partial_out.reshape(count, 2, half_width)]
    dot_general x1, matrix products: 6.33 us -> 10.2 us  [local(): jnp.einsum('md,fd->mf', cot, w_down, preferred_element_type=jnp.float32)]
    convert_element_type x3 -> x0, other arithmetic: 3.04 us -> none  [the longest x2 1.98 us: unit_rows(): (wide * lax.rsqrt(jnp.sum(wide * wide, axis=1, keepdims=True) + 1e-06)).a...]
    reduce_sum x3 -> x1, other arithmetic: 2.99 us -> 0.17 us  [local(): score_sel = jnp.sum(jnp.where(picked, shard_scores[None, :], 0.0), axis=1)]
  transfers between devices with their start and end apart: 16 -> 1, of which waited for: 6 -> 0; matrix products, arithmetic and copies ran while one was open for 8% -> 12% of each run, Pallas kernels for 0% -> 0%
where the time goes in v3:
time: 175 us
  Pallas kernels  119 us (68%)
  matrix products  25.9 us (15%)
  local copies, waits for them, and re-layouts  14.8 us (8%)
  other arithmetic  13.3 us (8%)
    pallas_call x1, Pallas kernels, gradients(): pl.pallas_call(kernel, out_shape=(jax.ShapeDtypeStruct((rows, hidden), jn...  93.7 us
    pallas_call x1, Pallas kernels, shard_learnability(): pl.pallas_call(kernel, out_shape=(jax.ShapeDtypeStruct((2,) + tile, jnp.f...  25.6 us
    dot_general x1, matrix products, local(): jnp.einsum('md,fd->mf', cot, w_down, preferred_element_type=jnp.float32)  10.2 us
    unnamed x35, local copies, waits for them, and re-layouts  9.72 us
    convert_element_type x1, other arithmetic, local(): weighted_act = (row_weight * act.astype(jnp.float32)).astype(jnp.bfloat16)  6.21 us
    dot_general x1, matrix products, local(): pre = jnp.dot(x, w_up, preferred_element_type=jnp.float32)  6.15 us
    dot_general x1, matrix products, local(): jnp.dot(placer, out, preferred_element_type=jnp.float32)  5.21 us
    dot_general x1, matrix products, down(): return jnp.dot(act, columns, preferred_element_type=jnp.float32)  4.34 us
  transfers between devices with their start and end apart: 1, of which 0 were waited for; matrix products, arithmetic and copies ran while one was open for 12% of the time, Pallas kernels for 0%

profile of v3, /device:TPU:0, one launch (start us, length us, event | category | flops | bytes accessed | tf_op | source)
XLA Modules:
  0.0 174.9 jit_solution(17427146535095550027)
XLA Ops:
  0.6 0.0 copy-start
  0.6 0.0 copy-start.6
  0.7 0.0 copy-start.4
  0.7 0.0 copy-start.5
  0.7 0.8 compare_select_fusion
  1.5 0.4 copy-done
  1.9 0.6 gather_fusion
  2.5 1.8 %gather_fusion.1 = bf16[64,8,512]{2,1,0:T(8,128)(2,1)S(1)} fusion(bf16[128,8,512]{2,1,0:T(8,128)(2,1)} %param.16, s32[1024]{0:T(1024)S(1)} %pad_clamp_fusion), kind=kCustom, calls=%fused_computation.1 | custom fusion | bytes 1048832 | tf_op jit(solution)/shard_map/gather | solution.py:372
  4.3 1.0 copy.31
  5.3 1.0 copy.35
  6.3 0.0 copy-done.6
  6.3 0.0 copy-done.4
  6.3 0.0 copy-done.5
  6.3 0.9 copy-done.7
  7.2 25.6 %pair_losses.1 = (f32[2,8,128]{2,1,0:T(8,128)S(1)}, bf16[512,512]{1,0:T(8,128)(2,1)S(1)}, bf16[512,512]{1,0:T(8,128)(2,1)S(1)}) custom-call(bf16[64,768]{1,0:T(8,128)(2,1)S(1)} %copy-done.6, bf16[64,768]{1,0:T(8,128)(2,1)S(1)} %copy-done.7, bf16[64,1024]{1,0:T(8,128)(2,1)S(1)} %copy-done.4, bf16[64,1024]{1,0:T(8,128)(2,1)S(1)} %copy-done.5, ...), custom_call_target="tpu_custom_call" | custom-call | flops 268435456 | bytes 4194304 | tf_op jit(solution)/shard_map/pair_losses/pallas_call | solution.py:149
  32.8 0.2 copy.32
  33.0 0.2 copy.36
  33.3 0.0 copy-start.14
  33.3 2.5 %broadcast_select_fusion.1 = (bf16[512,512]{0,1:T(8,128)(2,1)}, bf16[512,512]{0,1:T(8,128)(2,1)}, bf16[512,512]{0,1:T(8,128)(2,1)S(1)}, bf16[512,512]{0,1:T(8,128)(2,1)S(1)}) fusion(bf16[512,512]{0,1:T(8,128)(2,1)} %copy.35, bf16[512,512]{0,1:T(8,128)(2,1)S(1)} %copy.36, pred[]{:T(512)S(6)} %eq.20, bf16[512,512]{0,1:T(8,128)(2,1)S(1)} %copy.32, ...), kind=kLoop, calls=%fused_computation.30 | loop fusion | flops 1048576 | bytes 4194305 | tf_op jit(solution)/shard_map/jit(_where)/select_n | solution.py:380
  35.7 0.2 copy-done.14
  35.9 6.2 %multiply_convert_fusion.1 = (bf16[512,2048]{1,0:T(8,128)(2,1)}, f32[512,2048]{1,0:T(8,128)}) fusion(bf16[1024,2048]{1,0:T(8,128)(2,1)S(1)} %copy-done.14, bf16[512,512]{0,1:T(8,128)(2,1)S(1)} %get-tuple-element.26, bf16[512,512]{0,1:T(8,128)(2,1)S(1)} %get-tuple-element.27), kind=kOutput, calls=%fused_computation.11 | convolution fusion | flops 2159017984 | bytes 11534336 | tf_op jit(solution)/shard_map/dot_general | solution.py:385
  42.1 0.0 copy-done.10
  42.1 0.0 copy-done.11
  42.1 4.3 %fusion.12 = bf16[512,512]{1,0:T(8,128)(2,1)} fusion(bf16[512,2048]{1,0:T(8,128)(2,1)} %get-tuple-element.24, bf16[2048,1024]{1,0:T(8,128)(2,1)} %param.18, s32[]{:T(128)S(6)} %select_n.67), kind=kOutput, calls=%fused_computation.20 | convolution fusion | flops 1074003968 | bytes 4718596 | tf_op jit(solution)/shard_map/dot_general | solution.py:390
  46.4 0.1 collective-permute-start
  46.5 1.3 fusion.19.refs_0_
  48.4 0.0 copy-done.12
  48.5 0.2 convert_reduce_fusion
  48.7 0.1 iota_add_fusion
  48.7 0.1 add.45
  48.8 2.1 %fusion.17.refs_1_ = bf16[1024,512]{1,0:T(8,128)(2,1)} fusion(bf16[512,512]{0,1:T(8,128)(2,1)} %get-tuple-element.19, bf16[512,512]{0,1:T(8,128)(2,1)S(1)} %copy-done.9), kind=kLoop, calls=%fused_computation.26 | loop fusion | flops 2097152 | bytes 2097152 | tf_op jit(solution)/shard_map/transpose | solution.py:433
  50.9 10.2 %fusion.5 = f32[512,2048]{1,0:T(8,128)} fusion(f32[512,2048]{1,0:T(8,128)} %get-tuple-element.25, bf16[2048,1024]{1,0:T(8,128)(2,1)} %param.18, bf16[512,512]{0,1:T(8,128)(2,1)} %get-tuple-element.19, bf16[512,512]{0,1:T(8,128)(2,1)S(1)} %copy-done.9), kind=kOutput, calls=%fused_computation.9 | convolution fusion | flops 2169503744 | bytes 13631488 | tf_op jit(solution)/shard_map/md,fd->mf/dot_general | solution.py:396
  61.2 0.1 pad_maximum_fusion.6
  61.2 0.0 copy-done.15
  61.3 0.2 select_reduce_fusion
  61.4 0.1 broadcast_in_dim.42
  61.5 0.1 mul.84
  61.6 6.2 %multiply_convert_fusion = (bf16[512,2048]{1,0:T(8,128)(2,1)}, bf16[512,2048]{1,0:T(8,128)(2,1)}) fusion(bf16[512,2048]{1,0:T(8,128)(2,1)} %get-tuple-element.24, f32[512]{0:T(512)S(1)} %mul.84, f32[512,2048]{1,0:T(8,128)} %fusion.5), kind=kLoop, calls=%fused_computation.10 | loop fusion | flops 5242880 | bytes 10487808 | tf_op jit(solution)/shard_map/convert_element_type | solution.py:431
  67.8 0.0 collective-permute-done
  67.8 5.2 %fusion.11 = bf16[1024,512]{1,0:T(8,128)(2,1)} fusion(s32[512]{0:T(512)S(1)} %add.45, bf16[512,512]{1,0:T(8,128)(2,1)} %collective-permute-done, bf16[512,2048]{1,0:T(8,128)(2,1)} %get-tuple-element.24, bf16[2048,1024]{1,0:T(8,128)(2,1)} %param.18, s32[]{:T(128)S(6)} %select_n.66, bf16[64,8,512]{2,1,0:T(8,128)(2,1)S(1)} %gather_fusion), kind=kOutput, calls=%fused_computation.19 | convolution fusion | flops 1612972032 | bytes 6293508 | tf_op jit(solution)/shard_map/dot_general | solution.py:412
  73.0 1.6 copy-done.1
  74.6 1.6 copy-done.2
  76.2 1.2 copy-done.3
  77.5 1.2 copy-done.8
  78.7 93.7 %grad_sums.1 = (f32[64,2048]{1,0:T(8,128)S(1)}, f32[64,2048]{1,0:T(8,128)S(1)}, bf16[8,128,512]{2,1,0:T(8,128)(2,1)S(1)}) custom-call(bf16[1024,512]{1,0:T(8,128)(2,1)S(1)} %fusion.19.refs_0_, bf16[1024,512]{1,0:T(8,128)(2,1)S(1)} %copy-done.3, bf16[512,2048]{1,0:T(8,128)(2,1)S(1)} %copy-done.2, bf16[512,2048]{1,0:T(8,128)(2,1)S(1)} %copy-done.1, ...), custom_call_target="tpu_custom_call" | custom-call | flops 4294967296 | bytes 16777216 | tf_op jit(solution)/shard_map/grad_sums/pallas_call | solution.py:314
  172.4 1.0 copy.43
  173.4 0.8 copy.44
  174.2 0.8 copy.45
  (19 shorter events, 0.1 us)
Async XLA Ops:
  0.6 1.2 copy-start
  0.6 5.7 %copy-start.6 = (bf16[64,768]{1,0:T(8,128)(2,1)S(1)}, bf16[64,768]{1,0:T(8,128)(2,1)}, u32[]{:S(2)}) copy-start(bf16[64,768]{1,0:T(8,128)(2,1)} %refs_0_.1) | copy-start | bytes 294916
  0.7 5.7 %copy-start.4 = (bf16[64,1024]{1,0:T(8,128)(2,1)S(1)}, bf16[64,1024]{1,0:T(8,128)(2,1)}, u32[]{:S(2)}) copy-start(bf16[64,1024]{1,0:T(8,128)(2,1)} %refs_2_.1) | copy-start | bytes 393220
  0.7 5.7 %copy-start.5 = (bf16[64,1024]{1,0:T(8,128)(2,1)S(1)}, bf16[64,1024]{1,0:T(8,128)(2,1)}, u32[]{:S(2)}) copy-start(bf16[64,1024]{1,0:T(8,128)(2,1)} %refs_3_.1) | copy-start | bytes 393220
  6.3 0.9 copy-start.7
  33.3 2.6 %copy-start.14 = (bf16[1024,2048]{1,0:T(8,128)(2,1)S(1)}, bf16[1024,2048]{1,0:T(8,128)(2,1)}, u32[]{:S(2)}) copy-start(bf16[1024,2048]{1,0:T(8,128)(2,1)} %param.17) | copy-start | bytes 12582916
  35.7 6.3 %copy-start.10 = (bf16[512,512]{0,1:T(8,128)(2,1)}, bf16[512,512]{0,1:T(8,128)(2,1)S(1)}, u32[]{:S(2)}) copy-start(bf16[512,512]{0,1:T(8,128)(2,1)S(1)} %get-tuple-element.26) | copy-start | bytes 1572868
  35.7 6.3 %copy-start.11 = (bf16[512,512]{0,1:T(8,128)(2,1)}, bf16[512,512]{0,1:T(8,128)(2,1)S(1)}, u32[]{:S(2)}) copy-start(bf16[512,512]{0,1:T(8,128)(2,1)S(1)} %get-tuple-element.27) | copy-start | bytes 1572868
  42.1 6.4 %copy-start.12 = (s32[64,1]{0,1:T(1,128)S(1)}, s32[64,1]{0,1:T(1,128)}, u32[]{:S(2)}) copy-start(s32[64,1]{0,1:T(1,128)} %param.21) | copy-start | bytes 772
  42.1 6.8 %copy-start.9 = (bf16[512,512]{0,1:T(8,128)(2,1)S(1)}, bf16[512,512]{0,1:T(8,128)(2,1)}, u32[]{:S(2)}) copy-start(bf16[512,512]{0,1:T(8,128)(2,1)} %get-tuple-element.18) | copy-start | bytes 1572868
  46.4 21.4 %collective-permute-start = (bf16[512,512]{1,0:T(8,128)(2,1)}, bf16[512,512]{1,0:T(8,128)(2,1)}, u32[]{:S(2)}, u32[]{:S(2)}) collective-permute-start(bf16[512,512]{1,0:T(8,128)(2,1)} %fusion.12), channel_id=1, source_target_pairs={{0,2},{2,0},{1,3},{3,1},{4,6},{6,4},{5,7},{7,5},{8,10},{10,8},{9,1... | collective-permute-start | bytes 1572872 | tf_op jit(solution)/shard_map/ppermute | solution.py:24
  50.9 10.3 %copy-start.15 = (s32[64]{0:T(128)S(1)}, s32[64]{0:T(128)}, u32[]{:S(2)}) copy-start(s32[64]{0:T(128)} %param.20) | copy-start | bytes 772
  61.2 6.7 %copy-start.13 = (f32[64]{0:T(128)}, f32[64]{0:T(128)S(1)}, u32[]{:S(2)}) copy-start(f32[64]{0:T(128)S(1)} %get-tuple-element.32) | copy-start | bytes 772
  73.0 1.6 copy-start.1
  74.6 1.6 copy-start.2
  76.2 1.2 copy-start.3
  77.5 1.2 copy-start.8

commit v4 on v3

--- a/solution.py
+++ b/solution.py
@@ -35,8 +35,8 @@
 
 def loss_kernel(
     n_dp, temp, bias,
-    ref_img, ref_txt, own_img, own_txt, half_x, half_cot,
-    score_ref, other_x, other_cot,
+    ref_img, ref_txt, own_img, own_txt, half_x, half_cot, up_ref, down_ref,
+    score_ref, wide_x, wide_cot, act_ref, grad_pre_ref,
     imgs, txts, row_out, row_in, text_out, text_in, share, share_in, send_sem, recv_sem,
 ):
     rows, width = own_img.shape
@@ -93,7 +93,34 @@
 
     copies = [send(txts.at[0], txts.at[m], to) for m, to in enumerate(across, 1)]
     copies += [send(imgs.at[0], imgs.at[m], to) for m, to in enumerate(near, 1)]
-    wide_copies = [send(half_x, other_x, over_tensor), send(half_cot, other_cot, over_tensor)]
+    half_width = half_x.shape[1]
+    columns = pl.ds(pl.multiple_of(tensor_at * half_width, half_width), half_width)
+    wide_copies = [
+        send(half_x, wide_x.at[:, columns], over_tensor),
+        send(half_cot, wide_cot.at[:, columns], over_tensor),
+    ]
+    wide_x[:, columns] = half_x[...]
+    wide_cot[:, columns] = half_cot[...]
+    for copy in wide_copies:
+        copy.wait()
+
+    def forward(step, carry):
+        tile = pl.ds(pl.multiple_of(step * 256, 256), 256)
+        h = jnp.dot(wide_x[...], up_ref[:, tile], preferred_element_type=jnp.float32)
+        back = lax.dot_general(
+            wide_cot[...], down_ref[tile, :], (((1,), (1,)), ((), ())),
+            preferred_element_type=jnp.float32,
+        )
+        slope = 0.7978845608028654
+        square = h * h
+        bend = jnp.tanh(slope * h * (1.0 + 0.044715 * square))
+        cdf = 0.5 * (1.0 + bend)
+        act_ref[:, tile] = (h * cdf).astype(jnp.bfloat16)
+        rise = cdf + 0.5 * h * (1.0 - bend * bend) * (slope * (1.0 + 0.134145 * square))
+        grad_pre_ref[:, tile] = (back * rise).astype(jnp.bfloat16)
+        return carry
+
+    lax.fori_loop(0, up_ref.shape[1] // 256, forward, 0)
     for copy in copies:
         copy.wait()
 
@@ -135,11 +162,11 @@
         mine = share[half] + share_in[0, 1 - half]
         partner = share_in[1, half] + share_in[2, 1 - half]
         score_ref[half] = jnp.where(group_at == 0, partner - mine, mine - partner)
-    for copy in wide_copies:
-        copy.wait()
-
-
-def shard_learnability(ref_img, ref_txt, own_img, own_txt, half_x, half_cot, n_dp):
+
+
+def shard_learnability(
+    ref_img, ref_txt, own_img, own_txt, half_x, half_cot, w_up, w_down, n_dp
+):
     rows, width = own_img.shape
     far = n_dp // 2
     copies = 3 + (far - 1) + 2 + 1 + (far - 1) + 3
@@ -150,11 +177,13 @@
         kernel,
         out_shape=(
             jax.ShapeDtypeStruct((2,) + tile, jnp.float32),
-            jax.ShapeDtypeStruct(half_x.shape, half_x.dtype),
-            jax.ShapeDtypeStruct(half_cot.shape, half_cot.dtype),
-        ),
-        in_specs=[vmem] * 6,
-        out_specs=(vmem, vmem, vmem),
+            jax.ShapeDtypeStruct((half_x.shape[0], w_up.shape[0]), half_x.dtype),
+            jax.ShapeDtypeStruct((half_x.shape[0], w_up.shape[0]), half_x.dtype),
+            jax.ShapeDtypeStruct((half_x.shape[0], w_up.shape[1]), jnp.bfloat16),
+            jax.ShapeDtypeStruct((half_x.shape[0], w_up.shape[1]), jnp.bfloat16),
+        ),
+        in_specs=[vmem] * 8,
+        out_specs=(vmem,) * 5,
         scratch_shapes=[
             pltpu.VMEM((4, rows, width), jnp.bfloat16),
             pltpu.VMEM((far, rows, width), jnp.bfloat16),
@@ -168,13 +197,13 @@
             pltpu.SemaphoreType.DMA((copies,)),
         ],
         compiler_params=pltpu.CompilerParams(
-            collective_id=1, has_side_effects=True, vmem_limit_bytes=24 * 1024 * 1024
+            collective_id=1, has_side_effects=True, vmem_limit_bytes=16 * 1024 * 1024
         ),
         cost_estimate=pl.CostEstimate(
             flops=16 * rows * rows * far * width, bytes_accessed=1 << 22, transcendentals=1 << 18
         ),
         name="pair_losses",
-    )(ref_img, ref_txt, own_img, own_txt, half_x, half_cot)
+    )(ref_img, ref_txt, own_img, own_txt, half_x, half_cot, w_up, w_down)
 
 
 def grad_kernel(
@@ -329,7 +358,7 @@
             pltpu.SemaphoreType.DMA((n_dp,)),
         ],
         compiler_params=pltpu.CompilerParams(
-            collective_id=0, has_side_effects=True, vmem_limit_bytes=44 * 1024 * 1024
+            collective_id=0, has_side_effects=True, vmem_limit_bytes=24 * 1024 * 1024
         ),
         cost_estimate=pl.CostEstimate(
             flops=4 * xt.shape[0] * depth * hidden, bytes_accessed=1 << 24, transcendentals=0
@@ -371,20 +400,10 @@
     half_x = patches[sel_index].reshape(count, half_width)
     half_cot = cotangent[sel_index].reshape(count, half_width)
 
-    scores, other_x, other_cot = shard_learnability(
-        ref_image, ref_text, learner_image, learner_text, half_x, half_cot, n_dp
-    )
-
-    def widen(half, other):
-        return jnp.concatenate(
-            [jnp.where(tensor_at == 0, half, other), jnp.where(tensor_at == 0, other, half)], axis=1
-        )
-
-    x = widen(half_x, other_x)
-    cot = widen(half_cot, other_cot)
-    pre = jnp.dot(x, w_up, preferred_element_type=jnp.float32)
-    act_full, gelu_back = jax.vjp(jax.nn.gelu, pre)
-    act = lax.optimization_barrier(act_full.astype(jnp.bfloat16))
+    scores, x, cot, act, grad_pre = shard_learnability(
+        ref_image, ref_text, learner_image, learner_text, half_x, half_cot, w_up, w_down, n_dp
+    )
+
     def down(side):
         columns = lax.dynamic_slice_in_dim(w_down, side * half_width, half_width, 1)
         return jnp.dot(act, columns, preferred_element_type=jnp.float32)
@@ -393,9 +412,6 @@
     out = (half_x.astype(jnp.float32) + (down(tensor_at) + came.astype(jnp.float32))).astype(
         jnp.bfloat16
     )
-    back = jnp.einsum("md,fd->mf", cot, w_down, preferred_element_type=jnp.float32)
-    grad_pre = lax.optimization_barrier(gelu_back(back)[0])
-
     live = jnp.arange(slots, dtype=jnp.int32) < counts[0]
     target = sel_dest[:, 0]
     earlier = jnp.arange(slots)[:, None] > jnp.arange(slots)[None, :]
@@ -427,7 +443,7 @@
     row_weight = jnp.repeat(weight, patch_rows)[:, None]
 
     axis_bits = [("dp", 1 << bit) for bit in range(n_dp.bit_length() - 2, -1, -1)] + [("group", 1)]
-    dh = (row_weight * grad_pre).astype(jnp.bfloat16)
+    dh = (row_weight * grad_pre.astype(jnp.float32)).astype(jnp.bfloat16)
     weighted_act = (row_weight * act.astype(jnp.float32)).astype(jnp.bfloat16)
     grad_up, grad_down_t, landed = gradients(
         x.T, cot.T, dh, weighted_act, boxed, axis_bits

time: 175 us -> 162 us (0.926)
  matrix products: 25.9 us -> 6.8 us
  local copies, waits for them, and re-layouts: 14.8 us -> 27.4 us
  other arithmetic: 13.3 us -> 6.34 us
    dot_general x2 -> x0, matrix products: 16.4 us -> none  [the longest x1 10.2 us: local(): jnp.einsum('md,fd->mf', cot, w_down, preferred_element_type=jnp.float32)]
    unnamed x35 -> x43, local copies, waits for them, and re-layouts: 9.72 us -> 18.6 us
    pallas_call x2, local copies, waits for them, and re-layouts: 0.43 us -> 4.57 us  [shard_learnability(): pl.pallas_call(kernel, out_shape=(jax.ShapeDtypeStruct((2,) + tile, jnp.f...]
    transpose x2 -> x0, other arithmetic: 3.35 us -> none  [local(): grad_up, grad_down_t, landed = gradients(x.T, cot.T, dh, weighted_act, bo...]
    select_n x1 -> x0, other arithmetic: 2.46 us -> none  [widen(): jnp.where(tensor_at == 0, half, other)]
    dot_general x1, matrix products: 4.34 us -> 2.07 us  [down(): return jnp.dot(act, columns, preferred_element_type=jnp.float32)]
    reshape x2 -> x0, local copies, waits for them, and re-layouts: 2.01 us -> none  [the longest x1 1 us: local(): half_x = patches[sel_index].reshape(count, half_width)]
  transfers between devices with their start and end apart: 1 -> 1, of which waited for: 0 -> 0; matrix products, arithmetic and copies ran while one was open for 12% -> 6% of each run, Pallas kernels for 0% -> 0%
where the time goes in v4:
time: 162 us; the launch traced here: 161 us
  Pallas kernels  119 us (73%)
  local copies, waits for them, and re-layouts  27.4 us (17%)
  matrix products  6.8 us (4%)
  other arithmetic  6.34 us (4%)
    pallas_call x1, Pallas kernels, gradients(): pl.pallas_call(kernel, out_shape=(jax.ShapeDtypeStruct((rows, hidden), jn...  93.6 us
    pallas_call x1, Pallas kernels, shard_learnability(): pl.pallas_call(kernel, out_shape=(jax.ShapeDtypeStruct((2,) + tile, jnp.f...  25.6 us
    unnamed x43, local copies, waits for them, and re-layouts  18.6 us
    convert_element_type x1, other arithmetic, local(): weighted_act = (row_weight * act.astype(jnp.float32)).astype(jnp.bfloat16)  5.04 us
    dot_general x1, matrix products, local(): jnp.dot(placer, out, preferred_element_type=jnp.float32)  4.72 us
    pallas_call x2, local copies, waits for them, and re-layouts, shard_learnability(): pl.pallas_call(kernel, out_shape=(jax.ShapeDtypeStruct((2,) + tile, jnp.f...  4.57 us
  transfers between devices with their start and end apart: 1, of which 0 were waited for; matrix products, arithmetic and copies ran while one was open for 6% of the time, Pallas kernels for 0%

profile of v4, /device:TPU:0, one launch (start us, length us, event | category | flops | bytes accessed | tf_op | source)
XLA Modules:
  0.0 161.2 jit_solution(6114021811240862578)
XLA Ops:
  0.6 0.0 copy-start
  0.6 0.0 copy-start.14
  0.7 0.0 copy-start.12
  0.7 0.0 copy-start.13
  0.7 0.8 compare_select_fusion
  1.5 0.4 copy-done
  1.9 1.4 gather_fusion
  3.3 2.6 %gather_fusion.1 = bf16[64,8,512]{2,1,0:T(8,128)(2,1)} fusion(bf16[128,8,512]{2,1,0:T(8,128)(2,1)} %param.16, s32[1024]{0:T(1024)S(1)} %pad_clamp_fusion), kind=kCustom, calls=%fused_computation.1 | custom fusion | bytes 1048832 | tf_op jit(solution)/shard_map/gather | solution.py:401
  5.9 0.0 copy-done.14
  5.9 0.0 copy-done.12
  5.9 0.0 copy-done.13
  5.9 0.0 copy-start.1
  5.9 2.2 %copy-done.1 = bf16[1024,2048]{1,0:T(8,128)(2,1)S(1)} copy-done((bf16[1024,2048]{1,0:T(8,128)(2,1)S(1)}, bf16[1024,2048]{1,0:T(8,128)(2,1)}, u32[]{:S(2)}) %copy-start.1) | copy-done | bytes 4194328
  8.1 2.2 %copy-done.2 = bf16[2048,1024]{1,0:T(8,128)(2,1)S(1)} copy-done((bf16[2048,1024]{1,0:T(8,128)(2,1)S(1)}, bf16[2048,1024]{1,0:T(8,128)(2,1)}, u32[]{:S(2)}) %copy-start.2) | copy-done | bytes 4194328
  10.3 1.0 copy-done.6
  11.3 1.0 copy-done.7
  12.4 0.9 copy-done.15
  13.2 25.6 %pair_losses.1 = (f32[2,8,128]{2,1,0:T(8,128)S(1)}, bf16[512,1024]{1,0:T(8,128)(2,1)S(1)}, bf16[512,1024]{1,0:T(8,128)(2,1)S(1)}, bf16[512,2048]{1,0:T(8,128)(2,1)S(1)}, bf16[512,2048]{1,0:T(8,128)(2,1)S(1)}) custom-call(bf16[64,768]{1,0:T(8,128)(2,1)S(1)} %copy-done.14, bf16[64,768]{1,0:T(8,128)(2,1)S(1)} %copy-done.15, bf16[64,1024]{1,0:T(8,128)(2,1)S(1)} %copy-done.12, ...), custom_call_target="tpu_custom_call" | custom-call | flops 268435456 | bytes 4194304 | tf_op jit(solution)/shard_map/pair_losses/pallas_call | solution.py:176
  38.8 0.0 copy-start.3
  38.8 1.3 copy-done.3
  40.2 2.1 %fusion.6 = bf16[512,512]{1,0:T(8,128)(2,1)} fusion(bf16[512,2048]{1,0:T(8,128)(2,1)S(1)} %get-tuple-element.16, bf16[2048,1024]{1,0:T(8,128)(2,1)S(1)} %copy-done.2, s32[]{:T(128)S(6)} %select_n.42), kind=kOutput, calls=%fused_computation.11 | convolution fusion | flops 1074003968 | bytes 4718596 | tf_op jit(solution)/shard_map/dot_general | solution.py:409
  42.3 0.0 copy-done.10
  42.3 0.0 copy-done.11
  42.3 0.1 collective-permute-start
  42.4 2.3 %copy.19 = bf16[512,1024]{0,1:T(8,128)(2,1)} copy(bf16[512,1024]{1,0:T(8,128)(2,1)} %copy-done.11) | data formatting | bytes 2097152 | tf_op jit(solution)/shard_map/pair_losses/pallas_call | solution.py:176
  44.7 2.3 %copy.20 = bf16[512,1024]{0,1:T(8,128)(2,1)} copy(bf16[512,1024]{1,0:T(8,128)(2,1)} %copy-done.10) | data formatting | bytes 2097152 | tf_op jit(solution)/shard_map/pair_losses/pallas_call | solution.py:176
  47.0 0.1 pad_maximum_fusion
  47.0 0.0 copy-done.19
  47.0 0.2 select_reduce_fusion
  47.9 0.1 broadcast_in_dim.42
  48.0 0.1 mul.40
  48.1 0.0 copy-done.17
  48.1 0.2 convert_reduce_fusion
  48.3 0.1 iota_add_fusion
  48.4 0.1 add.36
  48.5 5.0 %multiply_convert_fusion = (bf16[512,2048]{1,0:T(8,128)(2,1)}, bf16[512,2048]{1,0:T(8,128)(2,1)}) fusion(bf16[512,2048]{1,0:T(8,128)(2,1)S(1)} %get-tuple-element.16, f32[512]{0:T(512)S(1)} %mul.40, bf16[512,2048]{1,0:T(8,128)(2,1)} %copy-done.3), kind=kLoop, calls=%fused_computation.2 | loop fusion | flops 6291456 | bytes 8390656 | tf_op jit(solution)/shard_map/convert_element_type | solution.py:447
  53.5 0.0 copy-done.18
  53.5 0.0 collective-permute-done
  53.5 4.7 %fusion.5 = bf16[1024,512]{1,0:T(8,128)(2,1)} fusion(s32[512]{0:T(512)S(1)} %add.36, bf16[512,512]{1,0:T(8,128)(2,1)} %collective-permute-done, bf16[512,2048]{1,0:T(8,128)(2,1)S(1)} %get-tuple-element.16, bf16[2048,1024]{1,0:T(8,128)(2,1)} %refs_7_.1, s32[]{:T(128)S(6)} %select_n.41, bf16[64,8,512]{2,1,0:T(8,128)(2,1)} %gather_fusion), kind=kOutput, calls=%fused_computation.10 | convolution fusion | flops 1612972032 | bytes 6293508 | tf_op jit(solution)/shard_map/dot_general | solution.py:428
  58.2 1.6 copy-done.4
  59.8 1.6 copy-done.5
  61.4 1.2 copy-done.8
  62.6 1.2 copy-done.9
  63.9 1.2 copy-done.16
  65.1 93.6 %grad_sums.1 = (f32[64,2048]{1,0:T(8,128)S(1)}, f32[64,2048]{1,0:T(8,128)S(1)}, bf16[8,128,512]{2,1,0:T(8,128)(2,1)S(1)}) custom-call(bf16[1024,512]{1,0:T(8,128)(2,1)S(1)} %bitcast.26, bf16[1024,512]{1,0:T(8,128)(2,1)S(1)} %bitcast.27, bf16[512,2048]{1,0:T(8,128)(2,1)S(1)} %copy-done.5, bf16[512,2048]{1,0:T(8,128)(2,1)S(1)} %copy-done.4, ...), custom_call_target="tpu_custom_call" | custom-call | flops 4294967296 | bytes 16777216 | tf_op jit(solution)/shard_map/grad_sums/pallas_call | solution.py:343
  158.7 1.0 copy.25
  159.6 0.8 copy.26
  160.4 0.8 copy.27
  (20 shorter events, 0.1 us)
Async XLA Ops:
  0.6 1.2 copy-start
  0.6 5.2 %copy-start.14 = (bf16[64,768]{1,0:T(8,128)(2,1)S(1)}, bf16[64,768]{1,0:T(8,128)(2,1)}, u32[]{:S(2)}) copy-start(bf16[64,768]{1,0:T(8,128)(2,1)} %refs_0_.1) | copy-start | bytes 294916
  0.7 5.2 %copy-start.12 = (bf16[64,1024]{1,0:T(8,128)(2,1)S(1)}, bf16[64,1024]{1,0:T(8,128)(2,1)}, u32[]{:S(2)}) copy-start(bf16[64,1024]{1,0:T(8,128)(2,1)} %refs_2_.1) | copy-start | bytes 393220
  0.7 5.2 %copy-start.13 = (bf16[64,1024]{1,0:T(8,128)(2,1)S(1)}, bf16[64,1024]{1,0:T(8,128)(2,1)}, u32[]{:S(2)}) copy-start(bf16[64,1024]{1,0:T(8,128)(2,1)} %refs_3_.1) | copy-start | bytes 393220
  5.9 2.2 %copy-start.1 = (bf16[1024,2048]{1,0:T(8,128)(2,1)S(1)}, bf16[1024,2048]{1,0:T(8,128)(2,1)}, u32[]{:S(2)}) copy-start(bf16[1024,2048]{1,0:T(8,128)(2,1)} %refs_6_.1) | copy-start | bytes 12582916
  8.1 2.2 %copy-start.2 = (bf16[2048,1024]{1,0:T(8,128)(2,1)S(1)}, bf16[2048,1024]{1,0:T(8,128)(2,1)}, u32[]{:S(2)}) copy-start(bf16[2048,1024]{1,0:T(8,128)(2,1)} %refs_7_.1) | copy-start | bytes 12582916
  10.3 1.0 copy-start.6
  11.3 1.0 copy-start.7
  12.3 0.9 copy-start.15
  38.8 1.3 copy-start.3
  40.2 2.1 %copy-start.10 = (bf16[512,1024]{1,0:T(8,128)(2,1)}, bf16[512,1024]{1,0:T(8,128)(2,1)S(1)}, u32[]{:S(2)}) copy-start(bf16[512,1024]{1,0:T(8,128)(2,1)S(1)} %get-tuple-element.14) | copy-start | bytes 3145732
  40.2 2.1 %copy-start.11 = (bf16[512,1024]{1,0:T(8,128)(2,1)}, bf16[512,1024]{1,0:T(8,128)(2,1)S(1)}, u32[]{:S(2)}) copy-start(bf16[512,1024]{1,0:T(8,128)(2,1)S(1)} %get-tuple-element.13) | copy-start | bytes 3145732
  42.3 11.3 %collective-permute-start = (bf16[512,512]{1,0:T(8,128)(2,1)}, bf16[512,512]{1,0:T(8,128)(2,1)}, u32[]{:S(2)}, u32[]{:S(2)}) collective-permute-start(bf16[512,512]{1,0:T(8,128)(2,1)} %fusion.6), channel_id=1, source_target_pairs={{0,2},{2,0},{1,3},{3,1},{4,6},{6,4},{5,7},{7,5},{8,10},{10,8},{9,1... | collective-permute-start | bytes 1572872 | tf_op jit(solution)/shard_map/ppermute | solution.py:24
  42.4 4.7 %copy-start.19 = (s32[64]{0:T(128)S(1)}, s32[64]{0:T(128)}, u32[]{:S(2)}) copy-start(s32[64]{0:T(128)} %param.20) | copy-start | bytes 772
  42.4 5.7 %copy-start.17 = (s32[64,1]{0,1:T(1,128)S(1)}, s32[64,1]{0,1:T(1,128)}, u32[]{:S(2)}) copy-start(s32[64,1]{0,1:T(1,128)} %param.21) | copy-start | bytes 772
  47.0 6.5 %copy-start.18 = (f32[64]{0:T(128)}, f32[64]{0:T(128)S(1)}, u32[]{:S(2)}) copy-start(f32[64]{0:T(128)S(1)} %get-tuple-element.28) | copy-start | bytes 772
  58.2 1.6 copy-start.4
  59.8 1.6 copy-start.5
  61.4 1.2 copy-start.8
  62.6 1.2 copy-start.9
  63.9 1.2 copy-start.16

commit v5 on v4

--- a/solution.py
+++ b/solution.py
@@ -36,8 +36,8 @@
 def loss_kernel(
     n_dp, temp, bias,
     ref_img, ref_txt, own_img, own_txt, half_x, half_cot, up_ref, down_ref,
-    score_ref, wide_x, wide_cot, act_ref, grad_pre_ref,
-    imgs, txts, row_out, row_in, text_out, text_in, share, share_in, send_sem, recv_sem,
+    score_ref, xt_ref, ct_ref, act_ref, grad_pre_ref,
+    wide_x, wide_cot, imgs, txts, row_out, row_in, text_out, text_in, share, share_in, send_sem, recv_sem,
 ):
     rows, width = own_img.shape
     far = n_dp // 2
@@ -121,6 +121,8 @@
         return carry
 
     lax.fori_loop(0, up_ref.shape[1] // 256, forward, 0)
+    xt_ref[...] = wide_x[...].T
+    ct_ref[...] = wide_cot[...].T
     for copy in copies:
         copy.wait()
 
@@ -177,14 +179,16 @@
         kernel,
         out_shape=(
             jax.ShapeDtypeStruct((2,) + tile, jnp.float32),
-            jax.ShapeDtypeStruct((half_x.shape[0], w_up.shape[0]), half_x.dtype),
-            jax.ShapeDtypeStruct((half_x.shape[0], w_up.shape[0]), half_x.dtype),
+            jax.ShapeDtypeStruct((w_up.shape[0], half_x.shape[0]), half_x.dtype),
+            jax.ShapeDtypeStruct((w_up.shape[0], half_x.shape[0]), half_x.dtype),
             jax.ShapeDtypeStruct((half_x.shape[0], w_up.shape[1]), jnp.bfloat16),
             jax.ShapeDtypeStruct((half_x.shape[0], w_up.shape[1]), jnp.bfloat16),
         ),
         in_specs=[vmem] * 8,
         out_specs=(vmem,) * 5,
         scratch_shapes=[
+            pltpu.VMEM((half_x.shape[0], w_up.shape[0]), jnp.bfloat16),
+            pltpu.VMEM((half_x.shape[0], w_up.shape[0]), jnp.bfloat16),
             pltpu.VMEM((4, rows, width), jnp.bfloat16),
             pltpu.VMEM((far, rows, width), jnp.bfloat16),
             pltpu.VMEM((2,) + tile, jnp.float32),
@@ -400,7 +404,7 @@
     half_x = patches[sel_index].reshape(count, half_width)
     half_cot = cotangent[sel_index].reshape(count, half_width)
 
-    scores, x, cot, act, grad_pre = shard_learnability(
+    scores, xt, ct, act, grad_pre = shard_learnability(
         ref_image, ref_text, learner_image, learner_text, half_x, half_cot, w_up, w_down, n_dp
     )
 
@@ -446,7 +450,7 @@
     dh = (row_weight * grad_pre.astype(jnp.float32)).astype(jnp.bfloat16)
     weighted_act = (row_weight * act.astype(jnp.float32)).astype(jnp.bfloat16)
     grad_up, grad_down_t, landed = gradients(
-        x.T, cot.T, dh, weighted_act, boxed, axis_bits
+        xt, ct, dh, weighted_act, boxed, axis_bits
     )
     routed = landed.reshape(n_dp * cap, patch_rows, half_width)
     return (learnability, routed, grad_up, grad_down_t)

time: 162 us -> 157 us (0.969)
  local copies, waits for them, and re-layouts: 27.4 us -> 22.8 us
    pallas_call x2 -> x0, local copies, waits for them, and re-layouts: 4.57 us -> none  [shard_learnability(): pl.pallas_call(kernel, out_shape=(jax.ShapeDtypeStruct((2,) + tile, jnp.f...]
  transfers between devices with their start and end apart: 1 -> 1, of which waited for: 0 -> 0; matrix products, arithmetic and copies ran while one was open for 6% -> 4% of each run, Pallas kernels for 0% -> 0%
where the time goes in v5:
time: 157 us
  Pallas kernels  119 us (76%)
  local copies, waits for them, and re-layouts  22.8 us (15%)
  matrix products  6.8 us (4%)
  other arithmetic  6.34 us (4%)
    pallas_call x1, Pallas kernels, gradients(): pl.pallas_call(kernel, out_shape=(jax.ShapeDtypeStruct((rows, hidden), jn...  93.7 us
    pallas_call x1, Pallas kernels, shard_learnability(): pl.pallas_call(kernel, out_shape=(jax.ShapeDtypeStruct((2,) + tile, jnp.f...  25.6 us
    unnamed x43, local copies, waits for them, and re-layouts  18.6 us
    convert_element_type x1, other arithmetic, local(): weighted_act = (row_weight * act.astype(jnp.float32)).astype(jnp.bfloat16)  5.04 us
    dot_general x1, matrix products, local(): jnp.dot(placer, out, preferred_element_type=jnp.float32)  4.72 us
  transfers between devices with their start and end apart: 1, of which 0 were waited for; matrix products, arithmetic and copies ran while one was open for 4% of the time, Pallas kernels for 0%

profile of v5, /device:TPU:0, one launch (start us, length us, event | category | flops | bytes accessed | tf_op | source)
XLA Modules:
  0.0 156.8 jit_solution(15524943528843339010)
XLA Ops:
  0.6 0.0 copy-start
  0.6 0.0 copy-start.10
  0.7 0.0 copy-start.8
  0.7 0.0 copy-start.9
  0.7 0.8 compare_select_fusion
  1.5 0.4 copy-done
  1.9 1.4 gather_fusion
  3.3 2.6 %gather_fusion.1 = bf16[64,8,512]{2,1,0:T(8,128)(2,1)} fusion(bf16[128,8,512]{2,1,0:T(8,128)(2,1)} %param.16, s32[1024]{0:T(1024)S(1)} %pad_clamp_fusion), kind=kCustom, calls=%fused_computation.1 | custom fusion | bytes 1048832 | tf_op jit(solution)/shard_map/gather | solution.py:405
  5.9 0.0 copy-done.10
  5.9 0.0 copy-done.8
  5.9 0.0 copy-done.9
  5.9 0.0 copy-start.1
  5.9 2.2 %copy-done.1 = bf16[1024,2048]{1,0:T(8,128)(2,1)S(1)} copy-done((bf16[1024,2048]{1,0:T(8,128)(2,1)S(1)}, bf16[1024,2048]{1,0:T(8,128)(2,1)}, u32[]{:S(2)}) %copy-start.1) | copy-done | bytes 4194328
  8.1 0.0 copy-start.2
  8.1 2.2 %copy-done.2 = bf16[2048,1024]{1,0:T(8,128)(2,1)S(1)} copy-done((bf16[2048,1024]{1,0:T(8,128)(2,1)S(1)}, bf16[2048,1024]{1,0:T(8,128)(2,1)}, u32[]{:S(2)}) %copy-start.2) | copy-done | bytes 4194328
  10.3 0.0 copy-start.6
  10.3 1.0 copy-done.6
  11.3 1.0 copy-done.7
  12.4 0.9 copy-done.11
  13.2 25.6 %pair_losses.1 = (f32[2,8,128]{2,1,0:T(8,128)S(1)}, bf16[1024,512]{1,0:T(8,128)(2,1)S(1)}, bf16[1024,512]{1,0:T(8,128)(2,1)S(1)}, bf16[512,2048]{1,0:T(8,128)(2,1)S(1)}, bf16[512,2048]{1,0:T(8,128)(2,1)S(1)}) custom-call(bf16[64,768]{1,0:T(8,128)(2,1)S(1)} %copy-done.10, bf16[64,768]{1,0:T(8,128)(2,1)S(1)} %copy-done.11, bf16[64,1024]{1,0:T(8,128)(2,1)S(1)} %copy-done.8, ...), custom_call_target="tpu_custom_call" | custom-call | flops 268435456 | bytes 4194304 | tf_op jit(solution)/shard_map/pair_losses/pallas_call | solution.py:178
  38.8 0.0 copy-start.3
  38.8 1.3 copy-done.3
  40.2 2.1 %fusion.6 = bf16[512,512]{1,0:T(8,128)(2,1)} fusion(bf16[512,2048]{1,0:T(8,128)(2,1)S(1)} %get-tuple-element.16, bf16[2048,1024]{1,0:T(8,128)(2,1)S(1)} %copy-done.2, s32[]{:T(128)S(6)} %select_n.42), kind=kOutput, calls=%fused_computation.11 | convolution fusion | flops 1074003968 | bytes 4718596 | tf_op jit(solution)/shard_map/dot_general | solution.py:413
  42.3 0.0 copy-done.12
  42.3 0.0 copy-done.14
  42.3 0.1 collective-permute-start
  42.4 0.1 pad_maximum_fusion
  42.5 0.0 copy-done.19
  42.5 0.2 select_reduce_fusion
  43.3 0.1 broadcast_in_dim.42
  43.4 0.1 mul.40
  43.5 0.0 copy-done.17
  43.5 0.2 convert_reduce_fusion
  43.7 0.1 iota_add_fusion
  43.8 0.1 add.36
  43.9 5.0 %multiply_convert_fusion = (bf16[512,2048]{1,0:T(8,128)(2,1)}, bf16[512,2048]{1,0:T(8,128)(2,1)}) fusion(bf16[512,2048]{1,0:T(8,128)(2,1)S(1)} %get-tuple-element.16, f32[512]{0:T(512)S(1)} %mul.40, bf16[512,2048]{1,0:T(8,128)(2,1)} %copy-done.3), kind=kLoop, calls=%fused_computation.2 | loop fusion | flops 6291456 | bytes 8390656 | tf_op jit(solution)/shard_map/convert_element_type | solution.py:451
  48.9 0.0 copy-done.18
  48.9 0.0 collective-permute-done
  48.9 4.7 %fusion.5 = bf16[1024,512]{1,0:T(8,128)(2,1)} fusion(s32[512]{0:T(512)S(1)} %add.36, bf16[512,512]{1,0:T(8,128)(2,1)} %collective-permute-done, bf16[512,2048]{1,0:T(8,128)(2,1)S(1)} %get-tuple-element.16, bf16[2048,1024]{1,0:T(8,128)(2,1)} %refs_7_.1, s32[]{:T(128)S(6)} %select_n.41, bf16[64,8,512]{2,1,0:T(8,128)(2,1)} %gather_fusion), kind=kOutput, calls=%fused_computation.10 | convolution fusion | flops 1612972032 | bytes 6293508 | tf_op jit(solution)/shard_map/dot_general | solution.py:432
  53.7 1.6 %copy-done.4 = bf16[512,2048]{1,0:T(8,128)(2,1)S(1)} copy-done((bf16[512,2048]{1,0:T(8,128)(2,1)S(1)}, bf16[512,2048]{1,0:T(8,128)(2,1)}, u32[]{:S(2)}) %copy-start.4) | copy-done | bytes 2097176
  55.3 1.6 %copy-done.5 = bf16[512,2048]{1,0:T(8,128)(2,1)S(1)} copy-done((bf16[512,2048]{1,0:T(8,128)(2,1)S(1)}, bf16[512,2048]{1,0:T(8,128)(2,1)}, u32[]{:S(2)}) %copy-start.5) | copy-done | bytes 2097176
  56.9 1.2 copy-done.13
  58.1 1.2 copy-done.15
  59.3 1.2 copy-done.16
  60.5 93.7 %grad_sums.1 = (f32[64,2048]{1,0:T(8,128)S(1)}, f32[64,2048]{1,0:T(8,128)S(1)}, bf16[8,128,512]{2,1,0:T(8,128)(2,1)S(1)}) custom-call(bf16[1024,512]{1,0:T(8,128)(2,1)S(1)} %copy-done.13, bf16[1024,512]{1,0:T(8,128)(2,1)S(1)} %copy-done.15, bf16[512,2048]{1,0:T(8,128)(2,1)S(1)} %copy-done.5, bf16[512,2048]{1,0:T(8,128)(2,1)S(1)} %copy-done.4, ...), custom_call_target="tpu_custom_call" | custom-call | flops 4294967296 | bytes 16777216 | tf_op jit(solution)/shard_map/grad_sums/pallas_call | solution.py:347
  154.2 1.0 copy.19
  155.2 0.8 copy.20
  156.0 0.8 copy.21
  (18 shorter events, 0.1 us)
Async XLA Ops:
  0.6 1.2 copy-start
  0.6 5.2 %copy-start.10 = (bf16[64,768]{1,0:T(8,128)(2,1)S(1)}, bf16[64,768]{1,0:T(8,128)(2,1)}, u32[]{:S(2)}) copy-start(bf16[64,768]{1,0:T(8,128)(2,1)} %refs_0_.1) | copy-start | bytes 294916
  0.7 5.2 %copy-start.8 = (bf16[64,1024]{1,0:T(8,128)(2,1)S(1)}, bf16[64,1024]{1,0:T(8,128)(2,1)}, u32[]{:S(2)}) copy-start(bf16[64,1024]{1,0:T(8,128)(2,1)} %refs_2_.1) | copy-start | bytes 393220
  0.7 5.2 %copy-start.9 = (bf16[64,1024]{1,0:T(8,128)(2,1)S(1)}, bf16[64,1024]{1,0:T(8,128)(2,1)}, u32[]{:S(2)}) copy-start(bf16[64,1024]{1,0:T(8,128)(2,1)} %refs_3_.1) | copy-start | bytes 393220
  5.9 2.2 %copy-start.1 = (bf16[1024,2048]{1,0:T(8,128)(2,1)S(1)}, bf16[1024,2048]{1,0:T(8,128)(2,1)}, u32[]{:S(2)}) copy-start(bf16[1024,2048]{1,0:T(8,128)(2,1)} %refs_6_.1) | copy-start | bytes 12582916
  8.1 2.2 %copy-start.2 = (bf16[2048,1024]{1,0:T(8,128)(2,1)S(1)}, bf16[2048,1024]{1,0:T(8,128)(2,1)}, u32[]{:S(2)}) copy-start(bf16[2048,1024]{1,0:T(8,128)(2,1)} %refs_7_.1) | copy-start | bytes 12582916
  10.3 1.0 copy-start.6
  11.3 1.0 copy-start.7
  12.3 0.9 copy-start.11
  38.8 1.3 copy-start.3
  40.2 2.1 %copy-start.12 = (bf16[1024,512]{1,0:T(8,128)(2,1)}, bf16[1024,512]{1,0:T(8,128)(2,1)S(1)}, u32[]{:S(2)}) copy-start(bf16[1024,512]{1,0:T(8,128)(2,1)S(1)} %get-tuple-element.13.refs_0_) | copy-start | bytes 3145732
  40.2 2.1 %copy-start.14 = (bf16[1024,512]{1,0:T(8,128)(2,1)}, bf16[1024,512]{1,0:T(8,128)(2,1)S(1)}, u32[]{:S(2)}) copy-start(bf16[1024,512]{1,0:T(8,128)(2,1)S(1)} %get-tuple-element.14.refs_1_) | copy-start | bytes 3145732
  40.2 2.3 %copy-start.19 = (s32[64]{0:T(128)S(1)}, s32[64]{0:T(128)}, u32[]{:S(2)}) copy-start(s32[64]{0:T(128)} %param.20) | copy-start | bytes 772
  40.2 3.3 %copy-start.17 = (s32[64,1]{0,1:T(1,128)S(1)}, s32[64,1]{0,1:T(1,128)}, u32[]{:S(2)}) copy-start(s32[64,1]{0,1:T(1,128)} %param.21) | copy-start | bytes 772
  42.3 6.7 %collective-permute-start = (bf16[512,512]{1,0:T(8,128)(2,1)}, bf16[512,512]{1,0:T(8,128)(2,1)}, u32[]{:S(2)}, u32[]{:S(2)}) collective-permute-start(bf16[512,512]{1,0:T(8,128)(2,1)} %fusion.6), channel_id=1, source_target_pairs={{0,2},{2,0},{1,3},{3,1},{4,6},{6,4},{5,7},{7,5},{8,10},{10,8},{9,1... | collective-permute-start | bytes 1572872 | tf_op jit(solution)/shard_map/ppermute | solution.py:24
  42.4 6.5 %copy-start.18 = (f32[64]{0:T(128)}, f32[64]{0:T(128)S(1)}, u32[]{:S(2)}) copy-start(f32[64]{0:T(128)S(1)} %get-tuple-element.28) | copy-start | bytes 772
  53.7 1.6 %copy-start.4 = (bf16[512,2048]{1,0:T(8,128)(2,1)S(1)}, bf16[512,2048]{1,0:T(8,128)(2,1)}, u32[]{:S(2)}) copy-start(bf16[512,2048]{1,0:T(8,128)(2,1)} %get-tuple-element.22.refs_3_) | copy-start | bytes 6291460
  55.3 1.6 %copy-start.5 = (bf16[512,2048]{1,0:T(8,128)(2,1)S(1)}, bf16[512,2048]{1,0:T(8,128)(2,1)}, u32[]{:S(2)}) copy-start(bf16[512,2048]{1,0:T(8,128)(2,1)} %get-tuple-element.23.refs_2_) | copy-start | bytes 6291460
  56.9 1.2 copy-start.13
  58.1 1.2 copy-start.15
  59.3 1.2 copy-start.16
